TPU v7x, 512 devices: a whole 4x8x8 slice. The times are simulated.
512 devices in a mesh: ctx: 64 (over x, z, core), tp: 8 (over y).
Axes of the slice: x: 4, y: 8, z: 8, core: 2. Of those that a mesh axis runs over, the one named last changes fastest.
Arguments:
- queries: bfloat16 [16384, 4096], P(('ctx', 'tp')), may hold values from -8 to 8
- keys: bfloat16 [16384, 1024], P(('ctx', 'tp')), may hold values from -8 to 8
- values: bfloat16 [16384, 1024], P(('ctx', 'tp')), may hold values from -6 to 6
- grad_out: bfloat16 [16384, 4096], P(('ctx', 'tp')), may hold values from -6 to 6
- doc_lengths: int32 [24], replicated, may hold values from 1 to 2048, 16384 in all
Outputs:
- grad_queries: bfloat16 [16384, 4096], P(('ctx', 'tp'))
- grad_keys: bfloat16 [16384, 1024], P(('ctx', 'tp'))
- grad_values: bfloat16 [16384, 1024], P(('ctx', 'tp'))
Inputs may be any that keep to these rules, and one draw needn't show every extreme that they name: `doc_lengths`: whole documents in order; the lengths sum to 16384 and the longest has exactly 2048 tokens.
All inputs are finite; a program needn't handle non-finite values.
Results may differ from a plain program's by a relative error of at most 0.02.
Values may be sent and summed in bfloat16 or wider, within the bound.
A program may use at most 64 MiB of HBM per device.

v0:
```python
import jax
import jax.numpy as jnp
from jax import lax
from jax.sharding import PartitionSpec as P

HEAD = 128
SPAN = 8


def from_behind(value, axis, by):
    size = lax.axis_size(axis)
    pairs = [(i, i + by) for i in range(size) if 0 <= i + by < size]
    return lax.ppermute(value, axis, pairs)


def document_of(positions, doc_lengths):
    ends = jnp.cumsum(doc_lengths)
    found = jnp.sum((positions[:, None] >= ends[None, :]).astype(jnp.int32), axis=1)
    return jnp.where(positions >= 0, found, -1)


def shards(queries, keys, values, grad_out, doc_lengths):
    query_loc, key_loc, value_loc, cot_loc = (
        lax.all_to_all(queries, "tp", split_axis=1, concat_axis=0, tiled=True),
        lax.all_to_all(keys, "tp", split_axis=1, concat_axis=0, tiled=True),
        lax.all_to_all(values, "tp", split_axis=1, concat_axis=0, tiled=True),
        lax.all_to_all(grad_out, "tp", split_axis=1, concat_axis=0, tiled=True),
    )
    rows_here = query_loc.shape[0]
    kv_here = key_loc.shape[1] // HEAD
    group = query_loc.shape[1] // HEAD // kv_here
    factor = HEAD ** (-0.5)
    offset = lax.axis_index("ctx") * rows_here
    local_rows = jnp.arange(rows_here, dtype=jnp.int32)
    query_positions = offset + local_rows
    query_docs = document_of(query_positions, doc_lengths)

    def relay_step(carry, unused):
        moved = from_behind((carry[0], carry[1]), "ctx", 1)
        return (moved, moved)

    unused_last, (key_far, value_far) = lax.scan(
        relay_step, (key_loc, value_loc), None, length=SPAN
    )
    key_all = jnp.concatenate([key_loc[None], key_far], axis=0)
    value_all = jnp.concatenate([value_loc[None], value_far], axis=0)
    distances = jnp.arange(SPAN + 1, dtype=jnp.int32)
    query_four = query_loc.reshape(rows_here, kv_here, group, HEAD)
    cot_four = cot_loc.reshape(rows_here, kv_here, group, HEAD)

    def allowed_of(distance):
        key_positions = offset - distance * rows_here + local_rows
        key_docs = document_of(key_positions, doc_lengths)
        return (
            (query_docs[:, None] == key_docs[None, :])
            & (key_positions[None, :] <= query_positions[:, None])
            & (key_docs[None, :] >= 0)
        )

    def products(key_blk, value_blk):
        key_three = key_blk.reshape(rows_here, kv_here, HEAD)
        value_three = value_blk.reshape(rows_here, kv_here, HEAD)
        scores = (
            jnp.einsum("qngd,knd->ngqk", query_four, key_three, preferred_element_type=jnp.float32)
            * factor
        )
        dprobs = jnp.einsum(
            "qngd,knd->ngqk", cot_four, value_three, preferred_element_type=jnp.float32
        )
        return (key_three, scores, dprobs)

    def gather_stats(carry, items):
        key_blk, value_blk, distance = items
        allowed = allowed_of(distance)
        top, total, weighted = carry
        unused_keys, scores, dprobs = products(key_blk, value_blk)
        masked = jnp.where(allowed, scores, -1e30)
        new_top = jnp.maximum(top, jnp.max(masked, axis=-1))
        weights = jnp.where(allowed, jnp.exp(masked - new_top[..., None]), 0.0)
        shrink = jnp.exp(top - new_top)
        total = total * shrink + jnp.sum(weights, axis=-1)
        weighted = weighted * shrink + jnp.sum(weights * dprobs, axis=-1)
        return ((new_top, total, weighted), None)

    start_top = jnp.full((kv_here, group, rows_here), -1e30, jnp.float32)
    start_zero = jnp.zeros((kv_here, group, rows_here), jnp.float32)
    (top, total, weighted), unused_out = lax.scan(
        gather_stats, (start_top, start_zero, start_zero), (key_all, value_all, distances)
    )
    lse = top + jnp.log(total)
    delta = weighted / total

    def gradients(grad_q_acc, items):
        key_blk, value_blk, distance = items
        allowed = allowed_of(distance)
        accum = grad_q_acc
        key_three, scores, dprobs = products(key_blk, value_blk)
        probs = jnp.where(allowed, jnp.exp(jnp.where(allowed, scores, -1e30) - lse[..., None]), 0.0)
        probs_b = probs.astype(jnp.bfloat16)
        dscores_b = (probs * (dprobs - delta[..., None])).astype(jnp.bfloat16)
        accum = accum + jnp.einsum(
            "ngqk,knd->qngd", dscores_b, key_three, preferred_element_type=jnp.float32
        )
        grad_k = (
            jnp.einsum("ngqk,qngd->knd", dscores_b, query_four, preferred_element_type=jnp.float32)
            * factor
        )
        grad_v = jnp.einsum("ngqk,qngd->knd", probs_b, cot_four, preferred_element_type=jnp.float32)
        return (
            accum,
            (grad_k.reshape(rows_here, kv_here * HEAD), grad_v.reshape(rows_here, kv_here * HEAD)),
        )

    start_grad = jnp.zeros((rows_here, kv_here, group, HEAD), jnp.float32)
    grad_q_acc, (key_terms, value_terms) = lax.scan(
        gradients, start_grad, (key_all, value_all, distances)
    )
    grad_q_loc = (
        (grad_q_acc * factor).astype(jnp.bfloat16).reshape(rows_here, kv_here * group * HEAD)
    )

    def return_step(carry, items):
        moved_key, moved_value = (
            from_behind(carry[0].astype(jnp.bfloat16), "ctx", -1).astype(jnp.float32),
            from_behind(carry[1].astype(jnp.bfloat16), "ctx", -1).astype(jnp.float32),
        )
        return ((moved_key + items[0], moved_value + items[1]), None)

    start_pair = (key_terms[SPAN], value_terms[SPAN])
    ordered = (jnp.flip(key_terms[:SPAN], axis=0), jnp.flip(value_terms[:SPAN], axis=0))
    (key_total, value_total), unused_back = lax.scan(return_step, start_pair, ordered)
    grad_k_loc = key_total.astype(jnp.bfloat16)
    grad_v_loc = value_total.astype(jnp.bfloat16)
    grad_queries, grad_keys, grad_values = (
        lax.all_to_all(grad_q_loc, "tp", split_axis=0, concat_axis=1, tiled=True),
        lax.all_to_all(grad_k_loc, "tp", split_axis=0, concat_axis=1, tiled=True),
        lax.all_to_all(grad_v_loc, "tp", split_axis=0, concat_axis=1, tiled=True),
    )
    return (grad_queries, grad_keys, grad_values)


def solution(mesh):
    placed = (
        P(("ctx", "tp"), None),
        P(("ctx", "tp"), None),
        P(("ctx", "tp"), None),
        P(("ctx", "tp"), None),
        P(),
    )
    return jax.shard_map(
        shards,
        mesh=mesh,
        in_specs=placed,
        out_specs=(P(("ctx", "tp"), None), P(("ctx", "tp"), None), P(("ctx", "tp"), None)),
        check_vma=False,
    )
```

profile of v0, /device:TPU:6, one launch (start us, length us, event | category | flops | bytes accessed | tf_op | source)
XLA Modules:
  0.0 317.1 jit_solution(3908952497532223614)
XLA Ops:
  2.1 7.1 %all-to-all-start = ((bf16[32,8,128]{2,0,1:T(8,128)(2,1)}), bf16[32,8,128]{2,0,1:T(8,128)(2,1)S(1)}, u32[]{:S(2)}, u32[]{:S(2)}) async-start(bf16[32,8,128]{2,0,1:T(8,128)(2,1)} %copy_bitcast_fusion.5), calls=%async_computation | async-start | bytes 131072 | tf_op jit(solution)/shard_map/all_to_all | solution.py:25
  10.7 6.9 %all-to-all-done = bf16[32,8,128]{2,0,1:T(8,128)(2,1)S(1)} async-done(((bf16[32,8,128]{2,0,1:T(8,128)(2,1)}), bf16[32,8,128]{2,0,1:T(8,128)(2,1)S(1)}, u32[]{:S(2)}, u32[]{:S(2)}) %all-to-all-start) | async-done | bytes 65568 | tf_op jit(solution)/shard_map/all_to_all | solution.py:25
  17.6 3.4 %all-to-all-start.1 = ((bf16[32,8,128]{2,0,1:T(8,128)(2,1)}), bf16[32,8,128]{2,0,1:T(8,128)(2,1)S(1)}, u32[]{:S(2)}, u32[]{:S(2)}) async-start(bf16[32,8,128]{2,0,1:T(8,128)(2,1)} %copy_bitcast_fusion.4), calls=%async_computation.1 | async-start | bytes 131072 | tf_op jit(solution)/shard_map/all_to_all | solution.py:26
  22.6 6.6 %all-to-all-done.1 = bf16[32,8,128]{2,0,1:T(8,128)(2,1)S(1)} async-done(((bf16[32,8,128]{2,0,1:T(8,128)(2,1)}), bf16[32,8,128]{2,0,1:T(8,128)(2,1)S(1)}, u32[]{:S(2)}, u32[]{:S(2)}) %all-to-all-start.1) | async-done | bytes 65568 | tf_op jit(solution)/shard_map/all_to_all | solution.py:26
  29.3 3.4 %all-to-all-start.2 = ((bf16[32,8,512]{2,0,1:T(8,128)(2,1)}), bf16[32,8,512]{2,0,1:T(8,128)(2,1)S(1)}, u32[]{:S(2)}, u32[]{:S(2)}) async-start(bf16[32,8,512]{2,0,1:T(8,128)(2,1)} %bitcast.196), calls=%async_computation.2 | async-start | bytes 524288 | tf_op jit(solution)/shard_map/all_to_all | solution.py:24
  33.8 9.2 %all-to-all-done.2 = bf16[32,8,512]{2,0,1:T(8,128)(2,1)S(1)} async-done(((bf16[32,8,512]{2,0,1:T(8,128)(2,1)}), bf16[32,8,512]{2,0,1:T(8,128)(2,1)S(1)}, u32[]{:S(2)}, u32[]{:S(2)}) %all-to-all-start.2) | async-done | bytes 262176 | tf_op jit(solution)/shard_map/all_to_all | solution.py:24
  43.1 4.0 %all-to-all-start.3 = ((bf16[32,8,512]{2,0,1:T(8,128)(2,1)}), bf16[32,8,512]{2,0,1:T(8,128)(2,1)}, u32[]{:S(2)}, u32[]{:S(2)}) async-start(bf16[32,8,512]{2,0,1:T(8,128)(2,1)} %bitcast.195), calls=%async_computation.3 | async-start | bytes 524288 | tf_op jit(solution)/shard_map/all_to_all | solution.py:27
  47.1 88.4 %while.66 = (s32[]{:T(128)}, bf16[256,128]{1,0:T(8,128)(2,1)S(1)}, bf16[256,128]{1,0:T(8,128)(2,1)S(1)}, bf16[8,256,128]{2,1,0:T(8,128)(2,1)}, bf16[8,256,128]{2,1,0:T(8,128)(2,1)}, /*index=5*/s32[]{:T(128)}) while((s32[]{:T(128)}, bf16[256,128]{1,0:T(8,128)(2,1)S(1)}, bf16[256,128]{1,0:T(8,128)(2,1)S(1)}, bf16[8,256,128]{2,1,0:T(8,128)(2,1)}, ...), condition=%wide.region_1.2_spmd, body=%wide.region_0.0_spmd.sunk | while | flops 2 | bytes 1048741 | solution.py:42
  49.1 4.4 %collective-permute-start = (bf16[256,128]{1,0:T(8,128)(2,1)S(1)}, bf16[256,128]{1,0:T(8,128)(2,1)S(1)}, u32[]{:S(2)}, u32[]{:S(2)}) collective-permute-start(bf16[256,128]{1,0:T(8,128)(2,1)S(1)} %get-tuple-element.1110), channel_id=1, source_target_pairs={{0,8},{8,16},{16,24},{24,32},{32,40},{40,48},{48,56},{56,64},{64,7... | collective-permute-start | bytes 196616 | tf_op jit(solution)/shard_map/while/body/eval_jaxpr/ppermute | solution.py:13
  53.5 2.7 collective-permute-done.1
  63.2 3.8 %collective-permute-done.1 = bf16[256,128]{1,0:T(8,128)(2,1)S(1)} collective-permute-done((bf16[256,128]{1,0:T(8,128)(2,1)S(1)}, bf16[256,128]{1,0:T(8,128)(2,1)S(1)}, u32[]{:S(2)}, u32[]{:S(2)}) %collective-permute-start.1) | collective-permute-done | bytes 65568 | tf_op jit(solution)/shard_map/while/body/eval_jaxpr/ppermute | solution.py:13
  74.0 3.8 %collective-permute-done.1 = bf16[256,128]{1,0:T(8,128)(2,1)S(1)} collective-permute-done((bf16[256,128]{1,0:T(8,128)(2,1)S(1)}, bf16[256,128]{1,0:T(8,128)(2,1)S(1)}, u32[]{:S(2)}, u32[]{:S(2)}) %collective-permute-start.1) | collective-permute-done | bytes 65568 | tf_op jit(solution)/shard_map/while/body/eval_jaxpr/ppermute | solution.py:13
  84.9 3.8 %collective-permute-done.1 = bf16[256,128]{1,0:T(8,128)(2,1)S(1)} collective-permute-done((bf16[256,128]{1,0:T(8,128)(2,1)S(1)}, bf16[256,128]{1,0:T(8,128)(2,1)S(1)}, u32[]{:S(2)}, u32[]{:S(2)}) %collective-permute-start.1) | collective-permute-done | bytes 65568 | tf_op jit(solution)/shard_map/while/body/eval_jaxpr/ppermute | solution.py:13
  95.8 3.8 %collective-permute-done.1 = bf16[256,128]{1,0:T(8,128)(2,1)S(1)} collective-permute-done((bf16[256,128]{1,0:T(8,128)(2,1)S(1)}, bf16[256,128]{1,0:T(8,128)(2,1)S(1)}, u32[]{:S(2)}, u32[]{:S(2)}) %collective-permute-start.1) | collective-permute-done | bytes 65568 | tf_op jit(solution)/shard_map/while/body/eval_jaxpr/ppermute | solution.py:13
  106.7 3.8 %collective-permute-done.1 = bf16[256,128]{1,0:T(8,128)(2,1)S(1)} collective-permute-done((bf16[256,128]{1,0:T(8,128)(2,1)S(1)}, bf16[256,128]{1,0:T(8,128)(2,1)S(1)}, u32[]{:S(2)}, u32[]{:S(2)}) %collective-permute-start.1) | collective-permute-done | bytes 65568 | tf_op jit(solution)/shard_map/while/body/eval_jaxpr/ppermute | solution.py:13
  117.6 3.8 %collective-permute-done.1 = bf16[256,128]{1,0:T(8,128)(2,1)S(1)} collective-permute-done((bf16[256,128]{1,0:T(8,128)(2,1)S(1)}, bf16[256,128]{1,0:T(8,128)(2,1)S(1)}, u32[]{:S(2)}, u32[]{:S(2)}) %collective-permute-start.1) | collective-permute-done | bytes 65568 | tf_op jit(solution)/shard_map/while/body/eval_jaxpr/ppermute | solution.py:13
  128.4 3.8 %collective-permute-done.1 = bf16[256,128]{1,0:T(8,128)(2,1)S(1)} collective-permute-done((bf16[256,128]{1,0:T(8,128)(2,1)S(1)}, bf16[256,128]{1,0:T(8,128)(2,1)S(1)}, u32[]{:S(2)}, u32[]{:S(2)}) %collective-permute-start.1) | collective-permute-done | bytes 65568 | tf_op jit(solution)/shard_map/while/body/eval_jaxpr/ppermute | solution.py:13
  141.3 22.7 %while.68 = (s32[]{:T(128)}, f32[1,4,256]{2,1,0:T(4,128)S(1)}, f32[1,4,256]{2,1,0:T(4,128)S(1)}, f32[1,4,256]{2,1,0:T(4,128)S(1)}, s32[256]{0:T(256)S(1)}, /*ind...) while((s32[]{:T(128)}, f32[1,4,256]{2,1,0:T(4,128)S(1)}, ...), condition=%wide.region_9.10_spmd.clone.clone.clone, body=%wide.region_4.9_spmd.clone.clone.clone.sunk | while | flops 137128192 | bytes 4148024 | solution.py:87
  164.0 34.5 %while.69 = (s32[]{:T(128)}, f32[256,1,4,128]{0,3,2,1:T(8,128)S(1)}, f32[9,256,128]{2,1,0:T(8,128)}, f32[9,256,128]{2,1,0:T(8,128)S(1)}, bf16[9,256,128]{2,1,0:T...) while((s32[]{:T(128)}, ...), condition=%wide.region_12.13_spmd.clone.clone.clone, body=%wide.region_10.12_spmd.clone.clone.clone.sunk | while | flops 338218240 | bytes 7424851 | solution.py:115
  202.5 73.4 %while.67 = (s32[]{:T(128)}, bf16[256,128]{1,0:T(8,128)(2,1)S(1)}, bf16[256,128]{1,0:T(8,128)(2,1)}, f32[8,256,128]{2,1,0:T(8,128)S(1)}, f32[8,256,128]{2,1,0:T(8,128)}, /*index=5*/s32[]{:T(128)}) while((s32[]{:T(128)}, bf16[256,128]{1,0:T(8,128)(2,1)S(1)}, bf16[256,128]{1,0:T(8,128)(2,1)}, f32[8,256,128]{2,1,0:T(8,128)S(1)}, ...), condition=%wide.region_14.15_spmd, body=%wide.region_13.14_spmd.sunk | while | flops 196610 | bytes 1048741 | solution.py:131
  208.3 5.8 %collective-permute-start.3 = (bf16[256,128]{1,0:T(8,128)(2,1)}, bf16[256,128]{1,0:T(8,128)(2,1)S(1)}, u32[]{:S(2)}, u32[]{:S(2)}) collective-permute-start(bf16[256,128]{1,0:T(8,128)(2,1)} %get-tuple-element.1225), channel_id=1, source_target_pairs={{8,0},{16,8},{24,16},{32,24},{40,32},{48,40},{56,48},{64,56},{72,6... | collective-permute-start | bytes 196616 | tf_op jit(solution)/shard_map/while/body/eval_jaxpr/ppermute | solution.py:13
  218.0 5.8 %collective-permute-start.3 = (bf16[256,128]{1,0:T(8,128)(2,1)}, bf16[256,128]{1,0:T(8,128)(2,1)S(1)}, u32[]{:S(2)}, u32[]{:S(2)}) collective-permute-start(bf16[256,128]{1,0:T(8,128)(2,1)} %get-tuple-element.1225), channel_id=1, source_target_pairs={{8,0},{16,8},{24,16},{32,24},{40,32},{48,40},{56,48},{64,56},{72,6... | collective-permute-start | bytes 196616 | tf_op jit(solution)/shard_map/while/body/eval_jaxpr/ppermute | solution.py:13
  227.7 5.8 %collective-permute-start.3 = (bf16[256,128]{1,0:T(8,128)(2,1)}, bf16[256,128]{1,0:T(8,128)(2,1)S(1)}, u32[]{:S(2)}, u32[]{:S(2)}) collective-permute-start(bf16[256,128]{1,0:T(8,128)(2,1)} %get-tuple-element.1225), channel_id=1, source_target_pairs={{8,0},{16,8},{24,16},{32,24},{40,32},{48,40},{56,48},{64,56},{72,6... | collective-permute-start | bytes 196616 | tf_op jit(solution)/shard_map/while/body/eval_jaxpr/ppermute | solution.py:13
  237.3 5.8 %collective-permute-start.3 = (bf16[256,128]{1,0:T(8,128)(2,1)}, bf16[256,128]{1,0:T(8,128)(2,1)S(1)}, u32[]{:S(2)}, u32[]{:S(2)}) collective-permute-start(bf16[256,128]{1,0:T(8,128)(2,1)} %get-tuple-element.1225), channel_id=1, source_target_pairs={{8,0},{16,8},{24,16},{32,24},{40,32},{48,40},{56,48},{64,56},{72,6... | collective-permute-start | bytes 196616 | tf_op jit(solution)/shard_map/while/body/eval_jaxpr/ppermute | solution.py:13
  247.0 5.8 %collective-permute-start.3 = (bf16[256,128]{1,0:T(8,128)(2,1)}, bf16[256,128]{1,0:T(8,128)(2,1)S(1)}, u32[]{:S(2)}, u32[]{:S(2)}) collective-permute-start(bf16[256,128]{1,0:T(8,128)(2,1)} %get-tuple-element.1225), channel_id=1, source_target_pairs={{8,0},{16,8},{24,16},{32,24},{40,32},{48,40},{56,48},{64,56},{72,6... | collective-permute-start | bytes 196616 | tf_op jit(solution)/shard_map/while/body/eval_jaxpr/ppermute | solution.py:13
  256.6 5.8 %collective-permute-start.3 = (bf16[256,128]{1,0:T(8,128)(2,1)}, bf16[256,128]{1,0:T(8,128)(2,1)S(1)}, u32[]{:S(2)}, u32[]{:S(2)}) collective-permute-start(bf16[256,128]{1,0:T(8,128)(2,1)} %get-tuple-element.1225), channel_id=1, source_target_pairs={{8,0},{16,8},{24,16},{32,24},{40,32},{48,40},{56,48},{64,56},{72,6... | collective-permute-start | bytes 196616 | tf_op jit(solution)/shard_map/while/body/eval_jaxpr/ppermute | solution.py:13
  266.3 5.8 %collective-permute-start.3 = (bf16[256,128]{1,0:T(8,128)(2,1)}, bf16[256,128]{1,0:T(8,128)(2,1)S(1)}, u32[]{:S(2)}, u32[]{:S(2)}) collective-permute-start(bf16[256,128]{1,0:T(8,128)(2,1)} %get-tuple-element.1225), channel_id=1, source_target_pairs={{8,0},{16,8},{24,16},{32,24},{40,32},{48,40},{56,48},{64,56},{72,6... | collective-permute-start | bytes 196616 | tf_op jit(solution)/shard_map/while/body/eval_jaxpr/ppermute | solution.py:13
  275.9 15.0 %all_to_all.127 = bf16[8,32,128]{2,1,0:T(8,128)(2,1)S(1)} all-to-all(bf16[8,32,128]{2,1,0:T(8,128)(2,1)S(1)} %bitcast.278), channel_id=1, replica_groups=mesh['ctx'=64,'tp'=8] {'tp'}, dimensions={0} | all-to-all | bytes 131072 | tf_op jit(solution)/shard_map/all_to_all | solution.py:136
  290.9 3.4 %all-to-all-start.6 = ((bf16[8,32,128]{2,1,0:T(8,128)(2,1)}), bf16[8,32,128]{2,1,0:T(8,128)(2,1)S(1)}, u32[]{:S(2)}, u32[]{:S(2)}) async-start(bf16[8,32,128]{2,1,0:T(8,128)(2,1)} %bitcast.19), calls=%async_computation.6 | async-start | bytes 131072 | tf_op jit(solution)/shard_map/all_to_all | solution.py:137
  295.3 7.2 %all-to-all-done.6 = bf16[8,32,128]{2,1,0:T(8,128)(2,1)S(1)} async-done(((bf16[8,32,128]{2,1,0:T(8,128)(2,1)}), bf16[8,32,128]{2,1,0:T(8,128)(2,1)S(1)}, u32[]{:S(2)}, u32[]{:S(2)}) %all-to-all-start.6) | async-done | bytes 65568 | tf_op jit(solution)/shard_map/all_to_all | solution.py:137
  302.5 3.4 %all-to-all-start.4 = ((bf16[8,32,512]{2,1,0:T(8,128)(2,1)}), bf16[8,32,512]{2,1,0:T(8,128)(2,1)S(1)}, u32[]{:S(2)}, u32[]{:S(2)}) async-start(bf16[8,32,512]{2,1,0:T(8,128)(2,1)} %all_to_all.108), calls=%async_computation.4 | async-start | bytes 524288 | tf_op jit(solution)/shard_map/all_to_all | solution.py:135
  307.2 9.1 %all-to-all-done.4 = bf16[8,32,512]{2,1,0:T(8,128)(2,1)S(1)} async-done(((bf16[8,32,512]{2,1,0:T(8,128)(2,1)}), bf16[8,32,512]{2,1,0:T(8,128)(2,1)S(1)}, u32[]{:S(2)}, u32[]{:S(2)}) %all-to-all-start.4) | async-done | bytes 262176 | tf_op jit(solution)/shard_map/all_to_all | solution.py:135
  (330 shorter events, 149.7 us)
Async XLA Ops:
  2.1 15.5 %all-to-all-start = ((bf16[32,8,128]{2,0,1:T(8,128)(2,1)}), bf16[32,8,128]{2,0,1:T(8,128)(2,1)S(1)}, u32[]{:S(2)}, u32[]{:S(2)}) async-start(bf16[32,8,128]{2,0,1:T(8,128)(2,1)} %copy_bitcast_fusion.5), calls=%async_computation | async-start | bytes 131072 | tf_op jit(solution)/shard_map/all_to_all | solution.py:25
  17.6 11.7 %all-to-all-start.1 = ((bf16[32,8,128]{2,0,1:T(8,128)(2,1)}), bf16[32,8,128]{2,0,1:T(8,128)(2,1)S(1)}, u32[]{:S(2)}, u32[]{:S(2)}) async-start(bf16[32,8,128]{2,0,1:T(8,128)(2,1)} %copy_bitcast_fusion.4), calls=%async_computation.1 | async-start | bytes 131072 | tf_op jit(solution)/shard_map/all_to_all | solution.py:26
  29.3 13.8 %all-to-all-start.2 = ((bf16[32,8,512]{2,0,1:T(8,128)(2,1)}), bf16[32,8,512]{2,0,1:T(8,128)(2,1)S(1)}, u32[]{:S(2)}, u32[]{:S(2)}) async-start(bf16[32,8,512]{2,0,1:T(8,128)(2,1)} %bitcast.196), calls=%async_computation.2 | async-start | bytes 524288 | tf_op jit(solution)/shard_map/all_to_all | solution.py:24
  43.1 95.5 %all-to-all-start.3 = ((bf16[32,8,512]{2,0,1:T(8,128)(2,1)}), bf16[32,8,512]{2,0,1:T(8,128)(2,1)}, u32[]{:S(2)}, u32[]{:S(2)}) async-start(bf16[32,8,512]{2,0,1:T(8,128)(2,1)} %bitcast.195), calls=%async_computation.3 | async-start | bytes 524288 | tf_op jit(solution)/shard_map/all_to_all | solution.py:27
  47.1 9.0 %collective-permute-start.1 = (bf16[256,128]{1,0:T(8,128)(2,1)S(1)}, bf16[256,128]{1,0:T(8,128)(2,1)S(1)}, u32[]{:S(2)}, u32[]{:S(2)}) collective-permute-start(bf16[256,128]{1,0:T(8,128)(2,1)S(1)} %get-tuple-element.1111), channel_id=1, source_target_pairs={{0,8},{8,16},{16,24},{24,32},{32,40},{40,48},{48,56},{56,64},{64,7... | collective-permute-start | bytes 196616 | tf_op jit(solution)/shard_map/while/body/eval_jaxpr/ppermute | solution.py:13
  49.1 9.0 %collective-permute-start = (bf16[256,128]{1,0:T(8,128)(2,1)S(1)}, bf16[256,128]{1,0:T(8,128)(2,1)S(1)}, u32[]{:S(2)}, u32[]{:S(2)}) collective-permute-start(bf16[256,128]{1,0:T(8,128)(2,1)S(1)} %get-tuple-element.1110), channel_id=1, source_target_pairs={{0,8},{8,16},{16,24},{24,32},{32,40},{40,48},{48,56},{56,64},{64,7... | collective-permute-start | bytes 196616 | tf_op jit(solution)/shard_map/while/body/eval_jaxpr/ppermute | solution.py:13
  59.3 7.7 %collective-permute-start.1 = (bf16[256,128]{1,0:T(8,128)(2,1)S(1)}, bf16[256,128]{1,0:T(8,128)(2,1)S(1)}, u32[]{:S(2)}, u32[]{:S(2)}) collective-permute-start(bf16[256,128]{1,0:T(8,128)(2,1)S(1)} %get-tuple-element.1111), channel_id=1, source_target_pairs={{0,8},{8,16},{16,24},{24,32},{32,40},{40,48},{48,56},{56,64},{64,7... | collective-permute-start | bytes 196616 | tf_op jit(solution)/shard_map/while/body/eval_jaxpr/ppermute | solution.py:13
  61.2 7.7 %collective-permute-start = (bf16[256,128]{1,0:T(8,128)(2,1)S(1)}, bf16[256,128]{1,0:T(8,128)(2,1)S(1)}, u32[]{:S(2)}, u32[]{:S(2)}) collective-permute-start(bf16[256,128]{1,0:T(8,128)(2,1)S(1)} %get-tuple-element.1110), channel_id=1, source_target_pairs={{0,8},{8,16},{16,24},{24,32},{32,40},{40,48},{48,56},{56,64},{64,7... | collective-permute-start | bytes 196616 | tf_op jit(solution)/shard_map/while/body/eval_jaxpr/ppermute | solution.py:13
  70.2 7.7 %collective-permute-start.1 = (bf16[256,128]{1,0:T(8,128)(2,1)S(1)}, bf16[256,128]{1,0:T(8,128)(2,1)S(1)}, u32[]{:S(2)}, u32[]{:S(2)}) collective-permute-start(bf16[256,128]{1,0:T(8,128)(2,1)S(1)} %get-tuple-element.1111), channel_id=1, source_target_pairs={{0,8},{8,16},{16,24},{24,32},{32,40},{40,48},{48,56},{56,64},{64,7... | collective-permute-start | bytes 196616 | tf_op jit(solution)/shard_map/while/body/eval_jaxpr/ppermute | solution.py:13
  72.1 7.7 %collective-permute-start = (bf16[256,128]{1,0:T(8,128)(2,1)S(1)}, bf16[256,128]{1,0:T(8,128)(2,1)S(1)}, u32[]{:S(2)}, u32[]{:S(2)}) collective-permute-start(bf16[256,128]{1,0:T(8,128)(2,1)S(1)} %get-tuple-element.1110), channel_id=1, source_target_pairs={{0,8},{8,16},{16,24},{24,32},{32,40},{40,48},{48,56},{56,64},{64,7... | collective-permute-start | bytes 196616 | tf_op jit(solution)/shard_map/while/body/eval_jaxpr/ppermute | solution.py:13
  81.1 7.7 %collective-permute-start.1 = (bf16[256,128]{1,0:T(8,128)(2,1)S(1)}, bf16[256,128]{1,0:T(8,128)(2,1)S(1)}, u32[]{:S(2)}, u32[]{:S(2)}) collective-permute-start(bf16[256,128]{1,0:T(8,128)(2,1)S(1)} %get-tuple-element.1111), channel_id=1, source_target_pairs={{0,8},{8,16},{16,24},{24,32},{32,40},{40,48},{48,56},{56,64},{64,7... | collective-permute-start | bytes 196616 | tf_op jit(solution)/shard_map/while/body/eval_jaxpr/ppermute | solution.py:13
  83.0 7.7 %collective-permute-start = (bf16[256,128]{1,0:T(8,128)(2,1)S(1)}, bf16[256,128]{1,0:T(8,128)(2,1)S(1)}, u32[]{:S(2)}, u32[]{:S(2)}) collective-permute-start(bf16[256,128]{1,0:T(8,128)(2,1)S(1)} %get-tuple-element.1110), channel_id=1, source_target_pairs={{0,8},{8,16},{16,24},{24,32},{32,40},{40,48},{48,56},{56,64},{64,7... | collective-permute-start | bytes 196616 | tf_op jit(solution)/shard_map/while/body/eval_jaxpr/ppermute | solution.py:13
  92.0 7.7 %collective-permute-start.1 = (bf16[256,128]{1,0:T(8,128)(2,1)S(1)}, bf16[256,128]{1,0:T(8,128)(2,1)S(1)}, u32[]{:S(2)}, u32[]{:S(2)}) collective-permute-start(bf16[256,128]{1,0:T(8,128)(2,1)S(1)} %get-tuple-element.1111), channel_id=1, source_target_pairs={{0,8},{8,16},{16,24},{24,32},{32,40},{40,48},{48,56},{56,64},{64,7... | collective-permute-start | bytes 196616 | tf_op jit(solution)/shard_map/while/body/eval_jaxpr/ppermute | solution.py:13
  93.9 7.7 %collective-permute-start = (bf16[256,128]{1,0:T(8,128)(2,1)S(1)}, bf16[256,128]{1,0:T(8,128)(2,1)S(1)}, u32[]{:S(2)}, u32[]{:S(2)}) collective-permute-start(bf16[256,128]{1,0:T(8,128)(2,1)S(1)} %get-tuple-element.1110), channel_id=1, source_target_pairs={{0,8},{8,16},{16,24},{24,32},{32,40},{40,48},{48,56},{56,64},{64,7... | collective-permute-start | bytes 196616 | tf_op jit(solution)/shard_map/while/body/eval_jaxpr/ppermute | solution.py:13
  102.8 7.7 %collective-permute-start.1 = (bf16[256,128]{1,0:T(8,128)(2,1)S(1)}, bf16[256,128]{1,0:T(8,128)(2,1)S(1)}, u32[]{:S(2)}, u32[]{:S(2)}) collective-permute-start(bf16[256,128]{1,0:T(8,128)(2,1)S(1)} %get-tuple-element.1111), channel_id=1, source_target_pairs={{0,8},{8,16},{16,24},{24,32},{32,40},{40,48},{48,56},{56,64},{64,7... | collective-permute-start | bytes 196616 | tf_op jit(solution)/shard_map/while/body/eval_jaxpr/ppermute | solution.py:13
  104.8 7.7 %collective-permute-start = (bf16[256,128]{1,0:T(8,128)(2,1)S(1)}, bf16[256,128]{1,0:T(8,128)(2,1)S(1)}, u32[]{:S(2)}, u32[]{:S(2)}) collective-permute-start(bf16[256,128]{1,0:T(8,128)(2,1)S(1)} %get-tuple-element.1110), channel_id=1, source_target_pairs={{0,8},{8,16},{16,24},{24,32},{32,40},{40,48},{48,56},{56,64},{64,7... | collective-permute-start | bytes 196616 | tf_op jit(solution)/shard_map/while/body/eval_jaxpr/ppermute | solution.py:13
  113.7 7.7 %collective-permute-start.1 = (bf16[256,128]{1,0:T(8,128)(2,1)S(1)}, bf16[256,128]{1,0:T(8,128)(2,1)S(1)}, u32[]{:S(2)}, u32[]{:S(2)}) collective-permute-start(bf16[256,128]{1,0:T(8,128)(2,1)S(1)} %get-tuple-element.1111), channel_id=1, source_target_pairs={{0,8},{8,16},{16,24},{24,32},{32,40},{40,48},{48,56},{56,64},{64,7... | collective-permute-start | bytes 196616 | tf_op jit(solution)/shard_map/while/body/eval_jaxpr/ppermute | solution.py:13
  115.6 7.7 %collective-permute-start = (bf16[256,128]{1,0:T(8,128)(2,1)S(1)}, bf16[256,128]{1,0:T(8,128)(2,1)S(1)}, u32[]{:S(2)}, u32[]{:S(2)}) collective-permute-start(bf16[256,128]{1,0:T(8,128)(2,1)S(1)} %get-tuple-element.1110), channel_id=1, source_target_pairs={{0,8},{8,16},{16,24},{24,32},{32,40},{40,48},{48,56},{56,64},{64,7... | collective-permute-start | bytes 196616 | tf_op jit(solution)/shard_map/while/body/eval_jaxpr/ppermute | solution.py:13
  124.6 7.7 %collective-permute-start.1 = (bf16[256,128]{1,0:T(8,128)(2,1)S(1)}, bf16[256,128]{1,0:T(8,128)(2,1)S(1)}, u32[]{:S(2)}, u32[]{:S(2)}) collective-permute-start(bf16[256,128]{1,0:T(8,128)(2,1)S(1)} %get-tuple-element.1111), channel_id=1, source_target_pairs={{0,8},{8,16},{16,24},{24,32},{32,40},{40,48},{48,56},{56,64},{64,7... | collective-permute-start | bytes 196616 | tf_op jit(solution)/shard_map/while/body/eval_jaxpr/ppermute | solution.py:13
  126.5 7.7 %collective-permute-start = (bf16[256,128]{1,0:T(8,128)(2,1)S(1)}, bf16[256,128]{1,0:T(8,128)(2,1)S(1)}, u32[]{:S(2)}, u32[]{:S(2)}) collective-permute-start(bf16[256,128]{1,0:T(8,128)(2,1)S(1)} %get-tuple-element.1110), channel_id=1, source_target_pairs={{0,8},{8,16},{16,24},{24,32},{32,40},{40,48},{48,56},{56,64},{64,7... | collective-permute-start | bytes 196616 | tf_op jit(solution)/shard_map/while/body/eval_jaxpr/ppermute | solution.py:13
  202.6 4.1 %collective-permute-start.3 = (bf16[256,128]{1,0:T(8,128)(2,1)}, bf16[256,128]{1,0:T(8,128)(2,1)S(1)}, u32[]{:S(2)}, u32[]{:S(2)}) collective-permute-start(bf16[256,128]{1,0:T(8,128)(2,1)} %get-tuple-element.1225), channel_id=1, source_target_pairs={{8,0},{16,8},{24,16},{32,24},{40,32},{48,40},{56,48},{64,56},{72,6... | collective-permute-start | bytes 196616 | tf_op jit(solution)/shard_map/while/body/eval_jaxpr/ppermute | solution.py:13
  204.5 3.8 %collective-permute-start.2 = (bf16[256,128]{1,0:T(8,128)(2,1)S(1)}, bf16[256,128]{1,0:T(8,128)(2,1)S(1)}, u32[]{:S(2)}, u32[]{:S(2)}) collective-permute-start(bf16[256,128]{1,0:T(8,128)(2,1)S(1)} %get-tuple-element.1224), channel_id=1, source_target_pairs={{8,0},{16,8},{24,16},{32,24},{40,32},{48,40},{56,48},{64,56},{72,6... | collective-permute-start | bytes 196616 | tf_op jit(solution)/shard_map/while/body/eval_jaxpr/ppermute | solution.py:13
  208.3 8.0 %collective-permute-start.3 = (bf16[256,128]{1,0:T(8,128)(2,1)}, bf16[256,128]{1,0:T(8,128)(2,1)S(1)}, u32[]{:S(2)}, u32[]{:S(2)}) collective-permute-start(bf16[256,128]{1,0:T(8,128)(2,1)} %get-tuple-element.1225), channel_id=1, source_target_pairs={{8,0},{16,8},{24,16},{32,24},{40,32},{48,40},{56,48},{64,56},{72,6... | collective-permute-start | bytes 196616 | tf_op jit(solution)/shard_map/while/body/eval_jaxpr/ppermute | solution.py:13
  218.0 8.0 %collective-permute-start.3 = (bf16[256,128]{1,0:T(8,128)(2,1)}, bf16[256,128]{1,0:T(8,128)(2,1)S(1)}, u32[]{:S(2)}, u32[]{:S(2)}) collective-permute-start(bf16[256,128]{1,0:T(8,128)(2,1)} %get-tuple-element.1225), channel_id=1, source_target_pairs={{8,0},{16,8},{24,16},{32,24},{40,32},{48,40},{56,48},{64,56},{72,6... | collective-permute-start | bytes 196616 | tf_op jit(solution)/shard_map/while/body/eval_jaxpr/ppermute | solution.py:13
  227.7 8.0 %collective-permute-start.3 = (bf16[256,128]{1,0:T(8,128)(2,1)}, bf16[256,128]{1,0:T(8,128)(2,1)S(1)}, u32[]{:S(2)}, u32[]{:S(2)}) collective-permute-start(bf16[256,128]{1,0:T(8,128)(2,1)} %get-tuple-element.1225), channel_id=1, source_target_pairs={{8,0},{16,8},{24,16},{32,24},{40,32},{48,40},{56,48},{64,56},{72,6... | collective-permute-start | bytes 196616 | tf_op jit(solution)/shard_map/while/body/eval_jaxpr/ppermute | solution.py:13
  233.5 3.8 %collective-permute-start.2 = (bf16[256,128]{1,0:T(8,128)(2,1)S(1)}, bf16[256,128]{1,0:T(8,128)(2,1)S(1)}, u32[]{:S(2)}, u32[]{:S(2)}) collective-permute-start(bf16[256,128]{1,0:T(8,128)(2,1)S(1)} %get-tuple-element.1224), channel_id=1, source_target_pairs={{8,0},{16,8},{24,16},{32,24},{40,32},{48,40},{56,48},{64,56},{72,6... | collective-permute-start | bytes 196616 | tf_op jit(solution)/shard_map/while/body/eval_jaxpr/ppermute | solution.py:13
  237.3 8.0 %collective-permute-start.3 = (bf16[256,128]{1,0:T(8,128)(2,1)}, bf16[256,128]{1,0:T(8,128)(2,1)S(1)}, u32[]{:S(2)}, u32[]{:S(2)}) collective-permute-start(bf16[256,128]{1,0:T(8,128)(2,1)} %get-tuple-element.1225), channel_id=1, source_target_pairs={{8,0},{16,8},{24,16},{32,24},{40,32},{48,40},{56,48},{64,56},{72,6... | collective-permute-start | bytes 196616 | tf_op jit(solution)/shard_map/while/body/eval_jaxpr/ppermute | solution.py:13
  247.0 8.0 %collective-permute-start.3 = (bf16[256,128]{1,0:T(8,128)(2,1)}, bf16[256,128]{1,0:T(8,128)(2,1)S(1)}, u32[]{:S(2)}, u32[]{:S(2)}) collective-permute-start(bf16[256,128]{1,0:T(8,128)(2,1)} %get-tuple-element.1225), channel_id=1, source_target_pairs={{8,0},{16,8},{24,16},{32,24},{40,32},{48,40},{56,48},{64,56},{72,6... | collective-permute-start | bytes 196616 | tf_op jit(solution)/shard_map/while/body/eval_jaxpr/ppermute | solution.py:13
  256.6 8.0 %collective-permute-start.3 = (bf16[256,128]{1,0:T(8,128)(2,1)}, bf16[256,128]{1,0:T(8,128)(2,1)S(1)}, u32[]{:S(2)}, u32[]{:S(2)}) collective-permute-start(bf16[256,128]{1,0:T(8,128)(2,1)} %get-tuple-element.1225), channel_id=1, source_target_pairs={{8,0},{16,8},{24,16},{32,24},{40,32},{48,40},{56,48},{64,56},{72,6... | collective-permute-start | bytes 196616 | tf_op jit(solution)/shard_map/while/body/eval_jaxpr/ppermute | solution.py:13
  266.3 8.0 %collective-permute-start.3 = (bf16[256,128]{1,0:T(8,128)(2,1)}, bf16[256,128]{1,0:T(8,128)(2,1)S(1)}, u32[]{:S(2)}, u32[]{:S(2)}) collective-permute-start(bf16[256,128]{1,0:T(8,128)(2,1)} %get-tuple-element.1225), channel_id=1, source_target_pairs={{8,0},{16,8},{24,16},{32,24},{40,32},{48,40},{56,48},{64,56},{72,6... | collective-permute-start | bytes 196616 | tf_op jit(solution)/shard_map/while/body/eval_jaxpr/ppermute | solution.py:13
  290.9 11.6 %all-to-all-start.6 = ((bf16[8,32,128]{2,1,0:T(8,128)(2,1)}), bf16[8,32,128]{2,1,0:T(8,128)(2,1)S(1)}, u32[]{:S(2)}, u32[]{:S(2)}) async-start(bf16[8,32,128]{2,1,0:T(8,128)(2,1)} %bitcast.19), calls=%async_computation.6 | async-start | bytes 131072 | tf_op jit(solution)/shard_map/all_to_all | solution.py:137
  302.5 13.8 %all-to-all-start.4 = ((bf16[8,32,512]{2,1,0:T(8,128)(2,1)}), bf16[8,32,512]{2,1,0:T(8,128)(2,1)S(1)}, u32[]{:S(2)}, u32[]{:S(2)}) async-start(bf16[8,32,512]{2,1,0:T(8,128)(2,1)} %all_to_all.108), calls=%async_computation.4 | async-start | bytes 524288 | tf_op jit(solution)/shard_map/all_to_all | solution.py:135
  (9 other events, 87.3 us)
where the time goes:
time: 319 us; the launch traced here: 317 us
  starting transfers between devices  116 us (36%)
  waiting for transfers between devices  86.7 us (27%)
  local copies, waits for them, and re-layouts  37.6 us (12%)
  matrix products  26.8 us (8%)
  other arithmetic  21.2 us (7%)
  blocking collectives  15 us (5%)
  loops' own time  13.2 us (4%)
    ppermute x32, starting transfers between devices, from_behind(): return lax.ppermute(value, axis, pairs)  91 us
    ppermute x32, waiting for transfers between devices, from_behind(): return lax.ppermute(value, axis, pairs)  47.6 us
    all_to_all x1, blocking collectives, shards(): lax.all_to_all(grad_k_loc, 'tp', split_axis=0, concat_axis=1, tiled=True)  15 us
    add x16, other arithmetic, return_step(): return ((moved_key + items[0], moved_value + items[1]), None)  12.5 us
    dynamic_slice x18, local copies, waits for them, and re-layouts, shards(): lax.scan(gather_stats, (start_top, start_zero, start_zero), (key_all, val...  10.5 us
    dynamic_update_slice x16, local copies, waits for them, and re-layouts, shards(): lax.scan(relay_step, (key_loc, value_loc), None, length=SPAN)  10.1 us
    all_to_all x1, waiting for transfers between devices, shards(): lax.all_to_all(queries, 'tp', split_axis=1, concat_axis=0, tiled=True)  9.24 us
    all_to_all x1, waiting for transfers between devices, shards(): lax.all_to_all(grad_q_loc, 'tp', split_axis=0, concat_axis=1, tiled=True)  9.13 us
  transfers between devices with their start and end apart: 38, of which 37 were waited for; matrix products, arithmetic and copies ran while one was open for 10% of the time, Pallas kernels for 0%

commit v1 on v0

v1 whole, which is shorter than its diff:
```python
import functools

import jax
import jax.numpy as jnp
from jax import lax
from jax.experimental import pallas as pl
from jax.experimental.pallas import tpu as pltpu
from jax.sharding import PartitionSpec as P

HEAD = 128
FAR = 4
MESH = pl.DeviceIdType.MESH
LOG2E = 1.4426950408889634
LOW = -1e30

NT = (((1,), (1,)), ((), ()))


def dot(a, b, dims=(((1,), (0,)), ((), ()))):
    return lax.dot_general(a, b, dims, preferred_element_type=jnp.float32)


def kernel(
    q_in, k_in, v_in, c_in, lengths,
    gq_out, gk_out, gv_out,
    q_blk, c_blk, k_win, v_win, weights, dprobs, tops, starts,
    dq_acc, dq_out, own, sib_out, sib_in, back_out, back_in,
    in_send, in_recv, fwd_send, fwd_recv, pair_send, pair_recv,
    back_send, back_recv, term_send, term_recv, out_send, out_recv,
):
    n = lax.axis_size("tp")
    ring = lax.axis_size("ctx")
    me = lax.axis_index("ctx")
    y = lax.axis_index("tp")
    core = lax.rem(me, 2)
    after = lax.rem(me + 2, ring)
    before = lax.rem(me + ring - 2, ring)
    twin = me + 1 - 2 * core
    rows = q_in.shape[0]
    block = rows * n
    group = q_blk.shape[1] // HEAD
    wide = group * HEAD
    factor = HEAD ** -0.5
    scale = factor * LOG2E
    mine = 1 - core

    barrier = pltpu.get_barrier_semaphore()

    def greet(o, carry):
        pl.semaphore_signal(
            barrier, inc=1, device_id=(me, lax.rem(y + o, n)), device_id_type=MESH
        )
        return carry

    lax.fori_loop(1, n, greet, 0)
    for other in (after, before, twin):
        pl.semaphore_signal(barrier, inc=1, device_id=(other, y), device_id_type=MESH)
    pl.semaphore_wait(barrier, n + 2)

    here = pl.ds(pl.multiple_of(y * rows, rows), rows)

    def spread(index, src, width, dst):
        def send(o, carry):
            to = lax.rem(y + o, n)
            pltpu.make_async_remote_copy(
                src_ref=src.at[:, pl.ds(pl.multiple_of(to * width, width), width)],
                dst_ref=dst,
                send_sem=in_send.at[index],
                recv_sem=in_recv.at[index],
                device_id=(me, to),
                device_id_type=MESH,
            ).start()
            return carry

        lax.fori_loop(1, n, send, 0)
        pltpu.make_async_copy(
            src.at[:, pl.ds(pl.multiple_of(y * width, width), width)], dst, in_recv.at[index]
        ).start()

    spread(0, k_in, HEAD, k_win.at[mine, here, :])
    spread(1, v_in, HEAD, v_win.at[mine, here, :])
    spread(2, q_in, wide, q_blk.at[here, :])
    spread(3, c_in, wide, c_blk.at[here, :])

    def got(ref, sem):
        pltpu.make_async_copy(ref, ref, sem).wait()

    def forward(index, win, step):
        at = 2 * step + mine
        return pltpu.make_async_remote_copy(
            src_ref=win.at[at],
            dst_ref=win.at[at + 2],
            send_sem=fwd_send.at[step, index],
            recv_sem=fwd_recv.at[step, index],
            device_id=(after, y),
            device_id_type=MESH,
        )

    def share(index, win, step):
        at = 2 * step + mine
        return pltpu.make_async_remote_copy(
            src_ref=win.at[at],
            dst_ref=win.at[at],
            send_sem=pair_send.at[step, index],
            recv_sem=pair_recv.at[step, index],
            device_id=(twin, y),
            device_id_type=MESH,
        )

    wins = (k_win, v_win)
    for index, win in enumerate(wins):
        got(win.at[mine], in_recv.at[index])
        forward(index, win, 0).start()
        share(index, win, 0).start()

    position = me * block + lax.broadcasted_iota(jnp.int32, (1, block), 1)
    begin = jnp.zeros((1, block), jnp.int32)
    end = jnp.int32(0)
    for d in range(lengths.shape[0]):
        end = end + lengths[d]
        begin = jnp.where(position >= end, end, begin)
    starts[...] = begin
    key_row = lax.broadcasted_iota(jnp.int32, (block, block), 0)
    query_lane = lax.broadcasted_iota(jnp.int32, (block, block), 1)

    for step in range(1, FAR):
        for index, win in enumerate(wins):
            forward(index, win, step - 1).wait_recv()
            forward(index, win, step).start()
            share(index, win, step).start()

    got(q_blk, in_recv.at[2])
    got(c_blk, in_recv.at[3])

    def columns(h):
        return slice(h * HEAD, (h + 1) * HEAD)

    def scan_block(far, carry, diagonal):
        at = far + mine
        k = k_win[at]
        v = v_win[at]
        allowed = key_row >= starts[...] - (me - far) * block
        if diagonal:
            allowed = allowed & (key_row <= query_lane)
        new = []
        for h in range(group):
            s = dot(k, q_blk[:, columns(h)], NT)
            dp = dot(v, c_blk[:, columns(h)], NT)
            s = jnp.where(allowed, s, LOW)
            top = jnp.max(s, axis=0, keepdims=True)
            if not diagonal:
                top = jnp.maximum(top, carry[h][0])
            e = jnp.exp2(s * scale - top * scale)
            total = jnp.sum(e, axis=0, keepdims=True)
            weighted = jnp.sum(e * dp, axis=0, keepdims=True)
            if not diagonal:
                old, old_total, old_weighted = carry[h]
                shrink = jnp.exp2((old - top) * scale)
                total = total + old_total * shrink
                weighted = weighted + old_weighted * shrink
            weights[far * group + h] = e
            dprobs[far * group + h] = dp
            tops[far * group + h] = top
            new.append((top, total, weighted))
        return tuple(new)

    stats = scan_block(0, None, True)
    for step in range(FAR):
        for index, win in enumerate(wins):
            share(index, win, step).wait_recv()
    stats = lax.fori_loop(1, 2 * FAR - 1, lambda far, c: scan_block(far, c, False), stats)
    for index, win in enumerate(wins):
        forward(index, win, FAR - 1).wait_recv()
        share(index, win, FAR).start()
    for index, win in enumerate(wins):
        share(index, win, FAR).wait_recv()
    stats = lax.fori_loop(2 * FAR - 1, 2 * FAR + 1, lambda far, c: scan_block(far, c, False), stats)

    dq_acc[...] = jnp.zeros_like(dq_acc)

    def terms(far):
        at = far + mine
        k_t = k_win[at].T
        dk = jnp.zeros((block, HEAD), jnp.float32)
        dv = jnp.zeros((block, HEAD), jnp.float32)
        for h in range(group):
            top, total, weighted = stats[h]
            inv = 1.0 / total
            shrink = jnp.exp2((tops[far * group + h] - top) * scale) * inv
            p = weights[far * group + h] * shrink
            ds = (p * (dprobs[far * group + h] - weighted * inv)).astype(jnp.bfloat16)
            dv = dv + dot(p.astype(jnp.bfloat16), c_blk[:, columns(h)])
            dk = dk + dot(ds, q_blk[:, columns(h)])
            dq_acc[h] += dot(k_t, ds)
        return dk, dv

    def hand_over(index, step):
        return pltpu.make_async_remote_copy(
            src_ref=sib_out.at[step, index],
            dst_ref=sib_in.at[step, index],
            send_sem=term_send.at[step, index],
            recv_sem=term_recv.at[step, index],
            device_id=(twin, y),
            device_id_type=MESH,
        )

    def back(index, step):
        return pltpu.make_async_remote_copy(
            src_ref=back_out.at[step, index],
            dst_ref=back_in.at[step - 1, index],
            send_sem=back_send.at[step - 1, index],
            recv_sem=back_recv.at[step - 1, index],
            device_id=(before, y),
            device_id_type=MESH,
        )

    def gives(step):
        return (step >= 1 - core) & (step <= FAR - core)

    def takes(step):
        return (step >= core) & (step <= FAR - 1 + core)

    def make_terms(step):
        @pl.when(gives(step))
        def _():
            for index, term in enumerate(terms(2 * step - 1 + 2 * core)):
                sib_out[step, index] = term.astype(jnp.bfloat16)
                hand_over(index, step).start()

        for index, term in enumerate(terms(2 * step)):
            own[step, index] = term

    def collect(step):
        for index in range(2):
            @pl.when(takes(step))
            def _():
                hand_over(index, step).wait_recv()
                own[step, index] += sib_in[step, index].astype(jnp.float32)

            @pl.when(step < FAR)
            def _():
                back(index, step + 1).wait_recv()
                own[step, index] += back_in[step, index].astype(jnp.float32)

            if index == 0:
                sums = own[step, index] * jnp.where(step == 0, factor, 1.0)
            else:
                sums = own[step, index]
            back_out[step, index] = sums.astype(jnp.bfloat16)

            @pl.when(step > 0)
            def _():
                back(index, step).start()

    def make_step(i, carry):
        step = FAR - i
        make_terms(step)

        @pl.when(step == FAR)
        def _():
            collect(step)

        return carry

    lax.fori_loop(0, FAR + 1, make_step, 0)

    def deliver(index, src, width, dst):
        to_columns = dst.at[:, pl.ds(pl.multiple_of(y * width, width), width)]

        def send(o, carry):
            to = lax.rem(y + o, n)
            pltpu.make_async_remote_copy(
                src_ref=src.at[pl.ds(pl.multiple_of(to * rows, rows), rows), :],
                dst_ref=to_columns,
                send_sem=out_send.at[index],
                recv_sem=out_recv.at[index],
                device_id=(me, to),
                device_id_type=MESH,
            ).start()
            return carry

        lax.fori_loop(1, n, send, 0)
        pltpu.make_async_copy(src.at[here, :], to_columns, out_recv.at[index]).start()

    for h in range(group):
        dq_out[:, columns(h)] = (dq_acc[h] * factor).T.astype(jnp.bfloat16)
    deliver(0, dq_out, wide, gq_out)

    def collect_step(i, carry):
        collect(FAR - 1 - i)
        return carry

    lax.fori_loop(0, FAR, collect_step, 0)
    deliver(1, back_out.at[0, 0], HEAD, gk_out)
    deliver(2, back_out.at[0, 1], HEAD, gv_out)

    for index, ref in enumerate((gq_out, gk_out, gv_out)):
        got(ref, out_recv.at[index])

    for index, (ref, width) in enumerate(((k_in, HEAD), (v_in, HEAD), (q_in, wide), (c_in, wide))):
        got(ref.at[:, pl.ds(0, (n - 1) * width)], in_send.at[index])
    for index, ref in enumerate((dq_out, back_out.at[0, 0], back_out.at[0, 1])):
        got(ref.at[pl.ds(0, (n - 1) * rows), :], out_send.at[index])
    for index, win in enumerate(wins):
        for step in range(FAR):
            forward(index, win, step).wait_send()
            back(index, step + 1).wait_send()
        for step in range(FAR + 1):
            share(index, win, step).wait_send()

            @pl.when(gives(step))
            def _():
                hand_over(index, step).wait_send()


def shards(queries, keys, values, grad_out, doc_lengths):
    n = lax.axis_size("tp")
    rows = queries.shape[0]
    block = rows * n
    wide = queries.shape[1] // n
    group = wide // HEAD
    blocks = 2 * FAR + 1
    bf16, f32 = jnp.bfloat16, jnp.float32
    vmem = pltpu.VMEM
    dma = pltpu.SemaphoreType.DMA
    any_spec = pl.BlockSpec(memory_space=pl.ANY)
    return pl.pallas_call(
        kernel,
        out_shape=[
            jax.ShapeDtypeStruct(queries.shape, bf16),
            jax.ShapeDtypeStruct(keys.shape, bf16),
            jax.ShapeDtypeStruct(values.shape, bf16),
        ],
        in_specs=[any_spec] * 4 + [pl.BlockSpec(memory_space=pltpu.SMEM)],
        out_specs=[any_spec] * 3,
        scratch_shapes=[
            vmem((block, wide), bf16),
            vmem((block, wide), bf16),
            vmem((2 * FAR + 2, block, HEAD), bf16),
            vmem((2 * FAR + 2, block, HEAD), bf16),
            vmem((blocks * group, block, block), f32),
            vmem((blocks * group, block, block), f32),
            vmem((blocks * group, 1, block), f32),
            vmem((1, block), jnp.int32),
            vmem((group, HEAD, block), f32),
            vmem((block, wide), bf16),
            vmem((FAR + 1, 2, block, HEAD), f32),
            vmem((FAR + 1, 2, block, HEAD), bf16),
            vmem((FAR + 1, 2, block, HEAD), bf16),
            vmem((FAR + 1, 2, block, HEAD), bf16),
            vmem((FAR, 2, block, HEAD), bf16),
            dma((4,)),
            dma((4,)),
            dma((FAR, 2)),
            dma((FAR, 2)),
            dma((FAR + 1, 2)),
            dma((FAR + 1, 2)),
            dma((FAR, 2)),
            dma((FAR, 2)),
            dma((FAR + 1, 2)),
            dma((FAR + 1, 2)),
            dma((3,)),
            dma((3,)),
        ],
        compiler_params=pltpu.CompilerParams(
            collective_id=0, has_side_effects=True, vmem_limit_bytes=48 * 2**20
        ),
    )(queries, keys, values, grad_out, doc_lengths)


def solution(mesh):
    placed = P(("ctx", "tp"), None)
    return jax.shard_map(
        shards,
        mesh=mesh,
        in_specs=(placed,) * 4 + (P(),),
        out_specs=(placed,) * 3,
        check_vma=False,
    )
```

time: 319 us -> 73.8 us (0.23)
  the two profiles are of different devices: /device:TPU:6 before, /device:TPU:1 now
where the time goes in v1:
time: 73.8 us; the launch traced here: 73.5 us
  Pallas kernels  66.7 us (90%)
  local copies, waits for them, and re-layouts  6.19 us (8%)
    pallas_call x1, Pallas kernels, shards(): pl.pallas_call(kernel, out_shape=[jax.ShapeDtypeStruct(queries.shape, bf1...  66.7 us
    unnamed x13, local copies, waits for them, and re-layouts  6.19 us

profile of v1, /device:TPU:1, one launch (start us, length us, event | category | flops | bytes accessed | tf_op | source)
XLA Modules:
  0.0 73.5 jit_solution(12154039168625096864)
XLA Ops:
  0.6 0.0 copy-start
  0.6 0.9 %copy-done = bf16[32,4096]{1,0:T(8,128)(2,1)S(1)} copy-done((bf16[32,4096]{1,0:T(8,128)(2,1)S(1)}, bf16[32,4096]{1,0:T(8,128)(2,1)}, u32[]{:S(2)}) %copy-start) | copy-done | bytes 262168
  1.6 0.0 copy-start.1
  1.6 0.9 %copy-done.1 = bf16[32,4096]{1,0:T(8,128)(2,1)S(1)} copy-done((bf16[32,4096]{1,0:T(8,128)(2,1)S(1)}, bf16[32,4096]{1,0:T(8,128)(2,1)}, u32[]{:S(2)}) %copy-start.1) | copy-done | bytes 262168
  2.5 0.0 copy-start.2
  2.5 0.8 %copy-done.2 = bf16[32,1024]{1,0:T(8,128)(2,1)S(1)} copy-done((bf16[32,1024]{1,0:T(8,128)(2,1)S(1)}, bf16[32,1024]{1,0:T(8,128)(2,1)}, u32[]{:S(2)}) %copy-start.2) | copy-done | bytes 65560
  3.4 0.0 copy-start.3
  3.4 0.8 %copy-done.3 = bf16[32,1024]{1,0:T(8,128)(2,1)S(1)} copy-done((bf16[32,1024]{1,0:T(8,128)(2,1)S(1)}, bf16[32,1024]{1,0:T(8,128)(2,1)}, u32[]{:S(2)}) %copy-start.3) | copy-done | bytes 65560
  4.2 0.0 copy-start.4
  4.2 0.7 copy-done.4
  4.9 66.7 %shard_map.76 = (bf16[32,4096]{1,0:T(8,128)(2,1)S(1)}, bf16[32,1024]{1,0:T(8,128)(2,1)S(1)}, bf16[32,1024]{1,0:T(8,128)(2,1)S(1)}) custom-call(bf16[32,4096]{1,0:T(8,128)(2,1)S(1)} %copy-done, bf16[32,1024]{1,0:T(8,128)(2,1)S(1)} %copy-done.2, bf16[32,1024]{1,0:T(8,128)(2,1)S(1)} %copy-done.3, bf16[32,4096]{1,0:T(8,128)(2,1)S(1)} %copy-done.1, s32[24]{0:T(128)S(1)} %copy-done.4), custom_call_target="tpu_custom_call" | custom-call | tf_op jit(solution)/shard_map/pallas_call | solution.py:327
  71.5 0.7 copy.11
  72.2 0.6 copy.12
  72.9 0.6 copy.13
Async XLA Ops:
  0.6 1.0 %copy-start = (bf16[32,4096]{1,0:T(8,128)(2,1)S(1)}, bf16[32,4096]{1,0:T(8,128)(2,1)}, u32[]{:S(2)}) copy-start(bf16[32,4096]{1,0:T(8,128)(2,1)} %q_in.1) | copy-start | bytes 786436
  1.6 0.9 %copy-start.1 = (bf16[32,4096]{1,0:T(8,128)(2,1)S(1)}, bf16[32,4096]{1,0:T(8,128)(2,1)}, u32[]{:S(2)}) copy-start(bf16[32,4096]{1,0:T(8,128)(2,1)} %c_in.1) | copy-start | bytes 786436
  2.5 0.8 %copy-start.2 = (bf16[32,1024]{1,0:T(8,128)(2,1)S(1)}, bf16[32,1024]{1,0:T(8,128)(2,1)}, u32[]{:S(2)}) copy-start(bf16[32,1024]{1,0:T(8,128)(2,1)} %k_in.1) | copy-start | bytes 196612
  3.4 0.8 %copy-start.3 = (bf16[32,1024]{1,0:T(8,128)(2,1)S(1)}, bf16[32,1024]{1,0:T(8,128)(2,1)}, u32[]{:S(2)}) copy-start(bf16[32,1024]{1,0:T(8,128)(2,1)} %v_in.1) | copy-start | bytes 196612
  4.2 0.7 copy-start.4

commit v2 on v1

v2 whole, which is shorter than its diff:
```python
import functools

import jax
import jax.numpy as jnp
from jax import lax
from jax.experimental import pallas as pl
from jax.experimental.pallas import tpu as pltpu
from jax.sharding import PartitionSpec as P

HEAD = 128
FAR = 4
HALVES = 2
MESH = pl.DeviceIdType.MESH
LOG2E = 1.4426950408889634
LOW = -1e30

NT = (((1,), (1,)), ((), ()))


def dot(a, b, dims=(((1,), (0,)), ((), ()))):
    return lax.dot_general(a, b, dims, preferred_element_type=jnp.float32)


def kernel(
    q_in, k_in, v_in, c_in, lengths,
    gq_out, near_k, near_v, far_k, far_v,
    q_stage, k_stage, v_stage, c_stage,
    q_blk, c_blk, k_win, v_win, weights, dprobs, tops, starts,
    dq_acc, dq_out, own, sib_out, sib_in, back_out, back_in,
    stage_sem, in_send, in_recv, fwd_send, fwd_recv, pair_send, pair_recv,
    back_send, back_recv, term_send, term_recv, out_send, out_recv,
):
    n = lax.axis_size("tp")
    ring = lax.axis_size("ctx")
    me = lax.axis_index("ctx")
    y = lax.axis_index("tp")
    core = lax.rem(me, 2)
    after = lax.rem(me + 2, ring)
    before = lax.rem(me + ring - 2, ring)
    twin = me + 1 - 2 * core
    rows = q_in.shape[0]
    block = rows * n
    half = block // HALVES
    group = dq_out.shape[1] // HEAD
    wide = group * HEAD
    factor = HEAD ** -0.5
    scale = factor * LOG2E
    mine = 1 - core
    offsets = sorted(range(1, n), key=lambda o: -min(o, n - o))

    barrier = pltpu.get_barrier_semaphore()
    for o in offsets:
        pl.semaphore_signal(
            barrier, inc=1, device_id=(me, lax.rem(y + o, n)), device_id_type=MESH
        )
    for other in (after, before, twin):
        pl.semaphore_signal(barrier, inc=1, device_id=(other, y), device_id_type=MESH)

    staged = ((k_in, k_stage), (v_in, v_stage), (q_in, q_stage), (c_in, c_stage))
    for index, (src, dst) in enumerate(staged):
        pltpu.make_async_copy(src, dst, stage_sem.at[index]).start()

    position = me * block + lax.broadcasted_iota(jnp.int32, (1, block), 1)
    begin = jnp.zeros((1, block), jnp.int32)
    end = jnp.int32(0)
    for d in range(lengths.shape[0]):
        end = end + lengths[d]
        begin = jnp.where(position >= end, end, begin)
    starts[...] = begin
    key_row = lax.broadcasted_iota(jnp.int32, (block, block), 0)
    query_lane = lax.broadcasted_iota(jnp.int32, (block, block), 1)

    for index, (src, dst) in enumerate(staged):
        pltpu.make_async_copy(src, dst, stage_sem.at[index]).wait()
    pl.semaphore_wait(barrier, n + 2)

    here = pl.ds(pl.multiple_of(y * rows, rows), rows)

    def spread(index, src, stride, width, shift, dst):
        def of(p):
            return src.at[:, pl.ds(pl.multiple_of(p * stride + shift, HEAD), width)]

        for o in offsets:
            to = lax.rem(y + o, n)
            pltpu.make_async_remote_copy(
                src_ref=of(to),
                dst_ref=dst,
                send_sem=in_send.at[index],
                recv_sem=in_recv.at[index],
                device_id=(me, to),
                device_id_type=MESH,
            ).start()
        pltpu.make_async_copy(of(y), dst, in_recv.at[index]).start()

    pair = wide // 2
    spread(0, k_stage, HEAD, HEAD, 0, k_win.at[mine, here, :])
    spread(1, v_stage, HEAD, HEAD, 0, v_win.at[mine, here, :])
    for side in range(2):
        spread(2 + 2 * side, q_stage, wide, pair, side * pair, q_blk.at[side, here, :])
        spread(3 + 2 * side, c_stage, wide, pair, side * pair, c_blk.at[side, here, :])

    def got(ref, sem):
        pltpu.make_async_copy(ref, ref, sem).wait()

    wins = (k_win, v_win)
    pieces = [(index, part) for index in range(2) for part in range(HALVES)]

    def forward(piece, step):
        index, part = piece
        at = 2 * step + mine
        span = pl.ds(part * half, half)
        return pltpu.make_async_remote_copy(
            src_ref=wins[index].at[at, span],
            dst_ref=wins[index].at[at + 2, span],
            send_sem=fwd_send.at[step, index, part],
            recv_sem=fwd_recv.at[step, index, part],
            device_id=(after, y),
            device_id_type=MESH,
        )

    def share(piece, step):
        index, part = piece
        at = 2 * step + mine
        span = pl.ds(part * half, half)
        return pltpu.make_async_remote_copy(
            src_ref=wins[index].at[at, span],
            dst_ref=wins[index].at[at, span],
            send_sem=pair_send.at[step, index, part],
            recv_sem=pair_recv.at[step, index, part],
            device_id=(twin, y),
            device_id_type=MESH,
        )

    for index, win in enumerate(wins):
        got(win.at[mine], in_recv.at[index])
        for part in range(HALVES):
            forward((index, part), 0).start()
        for part in range(HALVES):
            share((index, part), 0).start()

    for step in range(1, FAR):
        for piece in pieces:
            forward(piece, step - 1).wait_recv()
            forward(piece, step).start()
            share(piece, step).start()

    def columns(h):
        return slice((h % 2) * HEAD, (h % 2 + 1) * HEAD)

    def queries_of(h):
        return q_blk[h // 2, :, columns(h)]

    def cotangents_of(h):
        return c_blk[h // 2, :, columns(h)]

    def scan_block(far, carry, heads, diagonal=False):
        at = far + mine
        k = k_win[at]
        v = v_win[at]
        allowed = key_row >= starts[...] - (me - far) * block
        if diagonal:
            allowed = allowed & (key_row <= query_lane)
        new = []
        for j, h in enumerate(heads):
            s = dot(k, queries_of(h), NT)
            dp = dot(v, cotangents_of(h), NT)
            s = jnp.where(allowed, s, LOW)
            top = jnp.max(s, axis=0, keepdims=True)
            if not diagonal:
                top = jnp.maximum(top, carry[j][0])
            e = jnp.exp2(s * scale - top * scale)
            total = jnp.sum(e, axis=0, keepdims=True)
            weighted = jnp.sum(e * dp, axis=0, keepdims=True)
            if not diagonal:
                old, old_total, old_weighted = carry[j]
                shrink = jnp.exp2((old - top) * scale)
                total = total + old_total * shrink
                weighted = weighted + old_weighted * shrink
            weights[far * group + h] = e
            dprobs[far * group + h] = dp
            tops[far * group + h] = top
            new.append((top, total, weighted))
        return tuple(new)

    def scan(first, last, carry, heads):
        return lax.fori_loop(first, last, lambda far, c: scan_block(far, c, heads), carry)

    sides = (tuple(range(group // 2)), tuple(range(group // 2, group)))
    got(q_blk.at[0], in_recv.at[2])
    got(c_blk.at[0], in_recv.at[3])
    stats = [scan_block(0, None, sides[0], True), None]
    for step in range(FAR):
        for piece in pieces:
            share(piece, step).wait_recv()
    stats[0] = scan(1, 2 * FAR - 1, stats[0], sides[0])
    for piece in pieces:
        forward(piece, FAR - 1).wait_recv()
        share(piece, FAR).start()
    got(q_blk.at[1], in_recv.at[4])
    got(c_blk.at[1], in_recv.at[5])
    stats[1] = scan_block(0, None, sides[1], True)
    stats[1] = scan(1, 2 * FAR - 1, stats[1], sides[1])
    for piece in pieces:
        share(piece, FAR).wait_recv()
    for side in range(2):
        stats[side] = scan(2 * FAR - 1, 2 * FAR + 1, stats[side], sides[side])
    stats = stats[0] + stats[1]

    dq_acc[...] = jnp.zeros_like(dq_acc)

    def terms(far):
        at = far + mine
        k_t = k_win[at].T
        dk = jnp.zeros((block, HEAD), jnp.float32)
        dv = jnp.zeros((block, HEAD), jnp.float32)
        for h in range(group):
            top, total, weighted = stats[h]
            inv = 1.0 / total
            shrink = jnp.exp2((tops[far * group + h] - top) * scale) * inv
            p = weights[far * group + h] * shrink
            ds = (p * (dprobs[far * group + h] - weighted * inv)).astype(jnp.bfloat16)
            dv = dv + dot(p.astype(jnp.bfloat16), cotangents_of(h))
            dk = dk + dot(ds, queries_of(h))
            dq_acc[h] += dot(k_t, ds)
        return dk, dv

    def hand_over(index, step):
        return pltpu.make_async_remote_copy(
            src_ref=sib_out.at[step, index],
            dst_ref=sib_in.at[step, index],
            send_sem=term_send.at[step, index],
            recv_sem=term_recv.at[step, index],
            device_id=(twin, y),
            device_id_type=MESH,
        )

    def back(piece, step):
        index, part = piece
        span = pl.ds(part * half, half)
        return pltpu.make_async_remote_copy(
            src_ref=back_out.at[step, index, span],
            dst_ref=back_in.at[step - 1, index, span],
            send_sem=back_send.at[step - 1, index, part],
            recv_sem=back_recv.at[step - 1, index, part],
            device_id=(before, y),
            device_id_type=MESH,
        )

    def gives(step):
        return (step >= 1 - core) & (step <= FAR - core)

    def takes(step):
        return (step >= core) & (step <= FAR - 1 + core)

    def make_terms(step):
        @pl.when(gives(step))
        def _():
            for index, term in enumerate(terms(2 * step - 1 + 2 * core)):
                sib_out[step, index] = term.astype(jnp.bfloat16)
                hand_over(index, step).start()

        for index, term in enumerate(terms(2 * step)):
            own[step, index] = term

    def take(step):
        @pl.when(takes(step))
        def _():
            for index in range(2):
                hand_over(index, step).wait_recv()
                own[step, index] += sib_in[step, index].astype(jnp.float32)

    def make_step(i, carry):
        step = FAR - i
        make_terms(step)

        @pl.when(step == FAR)
        def _():
            take(step)
            for index, part in pieces:
                span = pl.ds(part * half, half)
                back_out[step, index, span] = own[step, index, span].astype(jnp.bfloat16)
                back((index, part), step).start()

        return carry

    lax.fori_loop(0, FAR + 1, make_step, 0)

    mine_there = {
        HEAD: pl.ds(pl.multiple_of(y * HEAD, HEAD), HEAD),
        wide: pl.ds(pl.multiple_of(y * wide, wide), wide),
    }

    def deliver(index, src, width, dst, to_ctx, others):
        for o in others:
            to = lax.rem(y + o, n)
            pltpu.make_async_remote_copy(
                src_ref=src.at[pl.ds(pl.multiple_of(to * rows, rows), rows), :],
                dst_ref=dst.at[:, mine_there[width]],
                send_sem=out_send.at[index],
                recv_sem=out_recv.at[index],
                device_id=(to_ctx, to),
                device_id_type=MESH,
            ).start()
        if 0 not in others:
            pltpu.make_async_copy(
                src.at[here, :], dst.at[:, mine_there[width]], out_recv.at[index]
            ).start()

    for h in range(group):
        dq_out[:, h * HEAD : (h + 1) * HEAD] = (dq_acc[h] * factor).T.astype(jnp.bfloat16)
    deliver(0, dq_out, wide, gq_out, me, offsets)
    take(0)
    for index, dst in enumerate((near_k, near_v)):
        back_out[0, index] = own[0, index].astype(jnp.bfloat16)
        deliver(1 + index, back_out.at[0, index], HEAD, dst, me, offsets)

    for step in range(FAR - 1, 0, -1):
        take(step)
        for index, part in pieces:
            span = pl.ds(part * half, half)
            back((index, part), step + 1).wait_recv()
            sums = own[step, index, span] + back_in[step, index, span].astype(jnp.float32)
            back_out[step, index, span] = sums.astype(jnp.bfloat16)
            if step > 1:
                back((index, part), step).start()
            elif part == HALVES - 1:
                deliver(
                    3 + index, back_out.at[1, index], HEAD, (far_k, far_v)[index],
                    before, offsets + [0],
                )

    for index, ref in enumerate((gq_out, near_k, near_v, far_k, far_v)):
        got(ref, out_recv.at[index])

    sent = ((k_in, HEAD), (v_in, HEAD), (q_in, pair), (c_in, pair), (q_in, pair), (c_in, pair))
    for index, (ref, width) in enumerate(sent):
        got(ref.at[:, pl.ds(0, (n - 1) * width)], in_send.at[index])
    for index, ref in enumerate((dq_out, back_out.at[0, 0], back_out.at[0, 1])):
        got(ref.at[pl.ds(0, (n - 1) * rows), :], out_send.at[index])
    for index in range(2):
        got(back_out.at[1, index], out_send.at[3 + index])
    for piece in pieces:
        for step in range(FAR):
            forward(piece, step).wait_send()
            if step:
                back(piece, step + 1).wait_send()
        for step in range(FAR + 1):
            share(piece, step).wait_send()
    for step in range(FAR + 1):
        @pl.when(gives(step))
        def _():
            for index in range(2):
                hand_over(index, step).wait_send()


def shards(queries, keys, values, grad_out, doc_lengths):
    n = lax.axis_size("tp")
    rows = queries.shape[0]
    block = rows * n
    wide = queries.shape[1] // n
    group = wide // HEAD
    blocks = 2 * FAR + 1
    bf16, f32 = jnp.bfloat16, jnp.float32
    vmem = pltpu.VMEM
    dma = pltpu.SemaphoreType.DMA
    any_spec = pl.BlockSpec(memory_space=pl.ANY)
    like_q = jax.ShapeDtypeStruct(queries.shape, bf16)
    like_k = jax.ShapeDtypeStruct(keys.shape, bf16)
    grad_q, near_k, near_v, far_k, far_v = pl.pallas_call(
        kernel,
        out_shape=[like_q] + [like_k] * 4,
        in_specs=[any_spec] * 4 + [pl.BlockSpec(memory_space=pltpu.SMEM)],
        out_specs=[any_spec] * 5,
        scratch_shapes=[
            vmem(queries.shape, bf16),
            vmem(keys.shape, bf16),
            vmem(values.shape, bf16),
            vmem(grad_out.shape, bf16),
            vmem((2, block, wide // 2), bf16),
            vmem((2, block, wide // 2), bf16),
            vmem((2 * FAR + 2, block, HEAD), bf16),
            vmem((2 * FAR + 2, block, HEAD), bf16),
            vmem((blocks * group, block, block), f32),
            vmem((blocks * group, block, block), f32),
            vmem((blocks * group, 1, block), f32),
            vmem((1, block), jnp.int32),
            vmem((group, HEAD, block), f32),
            vmem((block, wide), bf16),
            vmem((FAR + 1, 2, block, HEAD), f32),
            vmem((FAR + 1, 2, block, HEAD), bf16),
            vmem((FAR + 1, 2, block, HEAD), bf16),
            vmem((FAR + 1, 2, block, HEAD), bf16),
            vmem((FAR, 2, block, HEAD), bf16),
            dma((4,)),
            dma((6,)),
            dma((6,)),
            dma((FAR, 2, HALVES)),
            dma((FAR, 2, HALVES)),
            dma((FAR + 1, 2, HALVES)),
            dma((FAR + 1, 2, HALVES)),
            dma((FAR, 2, HALVES)),
            dma((FAR, 2, HALVES)),
            dma((FAR + 1, 2)),
            dma((FAR + 1, 2)),
            dma((5,)),
            dma((5,)),
        ],
        compiler_params=pltpu.CompilerParams(
            collective_id=0, has_side_effects=True, vmem_limit_bytes=60 * 2**20
        ),
    )(queries, keys, values, grad_out, doc_lengths)
    grad_k = (near_k.astype(f32) + far_k.astype(f32)) * HEAD ** -0.5
    grad_v = near_v.astype(f32) + far_v.astype(f32)
    return grad_q, grad_k.astype(bf16), grad_v.astype(bf16)


def solution(mesh):
    placed = P(("ctx", "tp"), None)
    return jax.shard_map(
        shards,
        mesh=mesh,
        in_specs=(placed,) * 4 + (P(),),
        out_specs=(placed,) * 3,
        check_vma=False,
    )
```

time: 73.8 us -> 66.2 us (0.90)
  local copies, waits for them, and re-layouts: 6.19 us -> 0.71 us
  Pallas kernels: 66.7 us -> 63 us
  other arithmetic: 0 us -> 1.67 us
    unnamed x13 -> x3, local copies, waits for them, and re-layouts: 6.19 us -> 0.71 us
    pallas_call x1, Pallas kernels: 66.7 us -> 63 us  [shards(): pl.pallas_call(kernel, out_shape=[like_q] + [like_k] * 4, in_specs=[any_s...]
    convert_element_type x0 -> x1, other arithmetic: none -> 1.67 us  [shards(): return (grad_q, grad_k.astype(bf16), grad_v.astype(bf16))]
where the time goes in v2:
time: 66.2 us; the launch traced here: 66 us
  Pallas kernels  63 us (95%)
  other arithmetic  1.67 us (3%)
  local copies, waits for them, and re-layouts  0.71 us (1%)
    pallas_call x1, Pallas kernels, shards(): pl.pallas_call(kernel, out_shape=[like_q] + [like_k] * 4, in_specs=[any_s...  63 us
    convert_element_type x1, other arithmetic, shards(): return (grad_q, grad_k.astype(bf16), grad_v.astype(bf16))  1.67 us

profile of v2, /device:TPU:1, one launch (start us, length us, event | category | flops | bytes accessed | tf_op | source)
XLA Modules:
  0.0 66.0 jit_solution(5516725114182788299)
XLA Ops:
  0.6 63.0 %shard_map.76 = (bf16[32,4096]{1,0:T(8,128)(2,1)}, bf16[32,1024]{1,0:T(8,128)(2,1)}, bf16[32,1024]{1,0:T(8,128)(2,1)}, bf16[32,1024]{1,0:T(8,128)(2,1)}, bf16[32,1024]{1,0:T(8,128)(2,1)}) custom-call(bf16[32,4096]{1,0:T(8,128)(2,1)} %q_in.1, bf16[32,1024]{1,0:T(8,128)(2,1)} %k_in.1, bf16[32,1024]{1,0:T(8,128)(2,1)} %v_in.1, bf16[32,4096]{1,0:T(8,128)(2,1)} %c_in.1, ...), custom_call_target="tpu_custom_call" | custom-call | tf_op jit(solution)/shard_map/pallas_call | solution.py:369
  63.6 0.0 copy-start
  63.7 1.7 %add_convert_fusion = (bf16[32,1024]{1,0:T(8,128)(2,1)}, bf16[32,1024]{1,0:T(8,128)(2,1)}) fusion(bf16[32,1024]{1,0:T(8,128)(2,1)} %get-tuple-element.12, bf16[32,1024]{1,0:T(8,128)(2,1)} %get-tuple-element.11, bf16[32,1024]{1,0:T(8,128)(2,1)} %get-tuple-element.10, bf16[32,1024]{1,0:T(8,128)(2,1)} %get-tuple-element.9), kind=kLoop, calls=%fused_computation | loop fusion | flops 294912 | bytes 393216 | tf_op jit(solution)/shard_map/convert_element_type | solution.py:414
  65.3 0.0 copy-done
  65.3 0.7 %copy.9 = bf16[32,4096]{1,0:T(8,128)(2,1)} copy(bf16[32,4096]{1,0:T(8,128)(2,1)S(1)} %copy-done) | data formatting | bytes 524288
Async XLA Ops:
  63.6 1.7 %copy-start = (bf16[32,4096]{1,0:T(8,128)(2,1)S(1)}, bf16[32,4096]{1,0:T(8,128)(2,1)}, u32[]{:S(2)}) copy-start(bf16[32,4096]{1,0:T(8,128)(2,1)} %get-tuple-element.18) | copy-start | bytes 786436

commit v3 on v2

v3 whole, which is shorter than its diff:
```python
import jax
import jax.numpy as jnp
from jax import lax
from jax.experimental import pallas as pl
from jax.experimental.pallas import tpu as pltpu
from jax.sharding import PartitionSpec as P

HEAD = 128
FAR = 4
HALVES = 2
MESH = pl.DeviceIdType.MESH
LOG2E = 1.4426950408889634
LOW = -1e30

NT = (((1,), (1,)), ((), ()))


def dot(a, b, dims=(((1,), (0,)), ((), ()))):
    return lax.dot_general(a, b, dims, preferred_element_type=jnp.float32)


def kernel(
    q_in, k_in, v_in, c_in, lengths,
    gq_out, near_out, far_out,
    qc_stage, kv_stage, qc_blk, kv_win, weights, dprobs, tops, starts,
    dq_acc, dq_out, own, sib_out, sib_in, back_out, back_in,
    stage_sem, in_send, in_recv, fwd_send, fwd_recv, pair_send, pair_recv,
    back_send, back_recv, term_send, term_recv, out_send, out_recv,
):
    n = lax.axis_size("tp")
    ring = lax.axis_size("ctx")
    me = lax.axis_index("ctx")
    y = lax.axis_index("tp")
    core = lax.rem(me, 2)
    chip = me // 2
    last = ring // 2 - 1
    after = lax.rem(me + 2, ring)
    before = lax.rem(me + ring - 2, ring)
    twin = me + 1 - 2 * core
    rows = q_in.shape[0]
    block = rows * n
    half = block // HALVES
    wide = qc_blk.shape[2]
    group = wide // HEAD
    factor = HEAD ** -0.5
    scale = factor * LOG2E
    mine = 1 - core
    offsets = sorted(range(1, n), key=lambda o: -min(o, n - o))

    barrier = pltpu.get_barrier_semaphore()
    for o in offsets:
        pl.semaphore_signal(
            barrier, inc=1, device_id=(me, lax.rem(y + o, n)), device_id_type=MESH
        )
    for other in (before, twin):
        pl.semaphore_signal(barrier, inc=1, device_id=(other, y), device_id_type=MESH)

    staged = (
        (k_in, kv_stage.at[0]),
        (v_in, kv_stage.at[1]),
        (q_in, qc_stage.at[0]),
        (c_in, qc_stage.at[1]),
    )
    for index, (src, dst) in enumerate(staged):
        pltpu.make_async_copy(src, dst, stage_sem.at[index]).start()

    position = me * block + lax.broadcasted_iota(jnp.int32, (1, block), 1)
    begin = jnp.zeros((1, block), jnp.int32)
    end = jnp.int32(0)
    for d in range(lengths.shape[0]):
        end = end + lengths[d]
        begin = jnp.where(position >= end, end, begin)
    starts[...] = begin
    key_row = lax.broadcasted_iota(jnp.int32, (block, block), 0)
    query_lane = lax.broadcasted_iota(jnp.int32, (block, block), 1)
    dq_acc[...] = jnp.zeros_like(dq_acc)

    for step in range(1, FAR + 1):
        @pl.when(chip < step)
        def _():
            kv_win[2 * step : 2 * step + 2] = jnp.zeros((2, *kv_win.shape[1:]), kv_win.dtype)

    @pl.when(chip == last)
    def _():
        back_in[...] = jnp.zeros_like(back_in)


    for index, (src, dst) in enumerate(staged):
        pltpu.make_async_copy(src, dst, stage_sem.at[index]).wait()
    pl.semaphore_wait(barrier, n + 1)

    here = pl.ds(pl.multiple_of(y * rows, rows), rows)

    def spread(index, src, width, dst):
        def of(p):
            return src.at[:, :, pl.ds(pl.multiple_of(p * width, width), width)]

        for o in offsets:
            to = lax.rem(y + o, n)
            pltpu.make_async_remote_copy(
                src_ref=of(to),
                dst_ref=dst,
                send_sem=in_send.at[index],
                recv_sem=in_recv.at[index],
                device_id=(me, to),
                device_id_type=MESH,
            ).start()
        pltpu.make_async_copy(of(y), dst, in_recv.at[index]).start()

    spread(0, kv_stage, HEAD, kv_win.at[mine, :, here, :])
    for h in range(group):
        for o in offsets + [0]:
            to = lax.rem(y + o, n)
            src = qc_stage.at[:, :, pl.ds(pl.multiple_of(to * wide + h * HEAD, HEAD), HEAD)]
            dst = qc_blk.at[:, here, h * HEAD : (h + 1) * HEAD]
            if o:
                pltpu.make_async_remote_copy(
                    src_ref=src, dst_ref=dst, send_sem=in_send.at[1], recv_sem=in_recv.at[1],
                    device_id=(me, to), device_id_type=MESH,
                ).start()
            else:
                pltpu.make_async_copy(src, dst, in_recv.at[1]).start()

    def got(ref, sem):
        pltpu.make_async_copy(ref, ref, sem).wait()

    pieces = [(index, part) for index in range(2) for part in range(HALVES)]

    def forward(piece, step):
        index, part = piece
        at = 2 * step + mine
        span = pl.ds(part * half, half)
        return pltpu.make_async_remote_copy(
            src_ref=kv_win.at[at, index, span],
            dst_ref=kv_win.at[at + 2, index, span],
            send_sem=fwd_send.at[step, index, part],
            recv_sem=fwd_recv.at[step, index, part],
            device_id=(after, y),
            device_id_type=MESH,
        )

    def share(piece, step):
        index, part = piece
        at = 2 * step + mine
        span = pl.ds(part * half, half)
        return pltpu.make_async_remote_copy(
            src_ref=kv_win.at[at, index, span],
            dst_ref=kv_win.at[at, index, span],
            send_sem=pair_send.at[step, index, part],
            recv_sem=pair_recv.at[step, index, part],
            device_id=(twin, y),
            device_id_type=MESH,
        )

    def relay(step):
        @pl.when(chip >= step)
        def _():
            for piece in pieces:
                forward(piece, step - 1).wait_recv()
                if step < FAR:
                    @pl.when(chip < last)
                    def _():
                        forward(piece, step).start()

                share(piece, step).start()

    def shared(step):
        @pl.when(chip >= step)
        def _():
            for piece in pieces:
                share(piece, step).wait_recv()

    def of_head(index, h):
        return qc_blk[index, :, h * HEAD : (h + 1) * HEAD]

    def scan_block(far, carry, diagonal=False):
        at = far + mine
        k = kv_win[at, 0]
        v = kv_win[at, 1]
        allowed = key_row >= starts[...] - (me - far) * block
        if diagonal:
            allowed = allowed & (key_row <= query_lane)
        new = []
        for h in range(group):
            s = dot(k, of_head(0, h), NT)
            dp = dot(v, of_head(1, h), NT)
            s = jnp.where(allowed, s, LOW)
            top = jnp.max(s, axis=0, keepdims=True)
            if not diagonal:
                top = jnp.maximum(top, carry[h][0])
            e = jnp.exp2(s * scale - top * scale)
            total = jnp.sum(e, axis=0, keepdims=True)
            weighted = jnp.sum(e * dp, axis=0, keepdims=True)
            if not diagonal:
                old, old_total, old_weighted = carry[h]
                shrink = jnp.exp2((old - top) * scale)
                total = total + old_total * shrink
                weighted = weighted + old_weighted * shrink
            weights[far * group + h] = e
            dprobs[far * group + h] = dp
            tops[far * group + h] = top
            new.append((top, total, weighted))
        return tuple(new)

    def scan(first, last, carry):
        return lax.fori_loop(first, last + 1, scan_block, carry)

    got(kv_win.at[mine], in_recv.at[0])

    @pl.when(chip < last)
    def _():
        for piece in pieces:
            forward(piece, 0).start()

    for piece in pieces:
        share(piece, 0).start()
    for step in range(1, FAR):
        relay(step)
    got(qc_blk, in_recv.at[1])
    stats = scan_block(0, None, True)
    for step in range(FAR):
        shared(step)
    stats = scan(1, 2 * FAR - 2, stats)
    relay(FAR)
    stats = scan_block(2 * FAR, stats)
    shared(FAR)
    stats = scan_block(2 * FAR - 1, stats)

    def terms(far):
        at = far + mine
        k_t = kv_win[at, 0].T
        dk = jnp.zeros((block, HEAD), jnp.float32)
        dv = jnp.zeros((block, HEAD), jnp.float32)
        for h in range(group):
            top, total, weighted = stats[h]
            inv = 1.0 / total
            shrink = jnp.exp2((tops[far * group + h] - top) * scale) * inv
            p = weights[far * group + h] * shrink
            ds = (p * (dprobs[far * group + h] - weighted * inv)).astype(jnp.bfloat16)
            dv = dv + dot(p.astype(jnp.bfloat16), of_head(1, h))
            dk = dk + dot(ds, of_head(0, h))
            dq_acc[h] += dot(k_t, ds)
        return dk, dv

    def hand_over(step):
        return pltpu.make_async_remote_copy(
            src_ref=sib_out.at[step],
            dst_ref=sib_in.at[step],
            send_sem=term_send.at[step],
            recv_sem=term_recv.at[step],
            device_id=(twin, y),
            device_id_type=MESH,
        )

    def back(piece, step):
        index, part = piece
        span = pl.ds(part * half, half)
        return pltpu.make_async_remote_copy(
            src_ref=back_out.at[step, index, span],
            dst_ref=back_in.at[step - 1, index, span],
            send_sem=back_send.at[step - 1, index, part],
            recv_sem=back_recv.at[step - 1, index, part],
            device_id=(before, y),
            device_id_type=MESH,
        )

    def gives(step):
        return (step >= 1 - core) & (step <= FAR - core)

    def takes(step):
        return (step >= core) & (step <= FAR - 1 + core)

    def make_terms(step):
        @pl.when(gives(step))
        def _():
            for index, term in enumerate(terms(2 * step - 1 + 2 * core)):
                sib_out[step, index] = term.astype(jnp.bfloat16)
            hand_over(step).start()

        for index, term in enumerate(terms(2 * step)):
            own[step, index] = term

    def take(step):
        @pl.when(takes(step))
        def _():
            hand_over(step).wait_recv()
            own[step] += sib_in[step].astype(jnp.float32)

    def pass_on(step):
        @pl.when(chip >= step)
        def _():
            for index, part in pieces:
                span = pl.ds(part * half, half)
                sums = own[step, index, span]
                if step < FAR:
                    @pl.when(chip < last)
                    def _():
                        back((index, part), step + 1).wait_recv()

                    sums = sums + back_in[step, index, span].astype(jnp.float32)
                back_out[step, index, span] = sums.astype(jnp.bfloat16)
                if step > 1:
                    back((index, part), step).start()

    def make_step(i, carry):
        step = FAR - i
        make_terms(step)

        @pl.when(step == FAR - 1)
        def _():
            take(FAR)
            pass_on(FAR)

        return carry

    def deliver(index, src, dst, to_ctx, others):
        def at(p):
            rows_of = pl.ds(pl.multiple_of(p * rows, rows), rows)
            return src.at[:, rows_of, :] if len(src.shape) == 3 else src.at[rows_of, :]

        for o in others:
            to = lax.rem(y + o, n)
            pltpu.make_async_remote_copy(
                src_ref=at(to),
                dst_ref=dst.at[y],
                send_sem=out_send.at[index],
                recv_sem=out_recv.at[index],
                device_id=(to_ctx, to),
                device_id_type=MESH,
            ).start()
        if 0 not in others:
            pltpu.make_async_copy(at(y), dst.at[y], out_recv.at[index]).start()

    lax.fori_loop(0, FAR + 1, make_step, 0)
    take(3)
    pass_on(3)
    for h in range(group):
        dq_out[:, h * HEAD : (h + 1) * HEAD] = (dq_acc[h] * factor).T.astype(jnp.bfloat16)
    deliver(0, dq_out, gq_out, me, offsets)
    take(0)
    back_out[0] = own[0].astype(jnp.bfloat16)
    deliver(1, back_out.at[0], near_out, me, offsets)
    take(2)
    pass_on(2)
    take(1)
    pass_on(1)

    @pl.when(chip > 0)
    def _():
        deliver(2, back_out.at[1], far_out, before, offsets + [0])

    @pl.when(chip == last)
    def _():
        for p in range(n):
            pltpu.make_async_copy(
                back_in.at[0, :, p * rows : (p + 1) * rows], far_out.at[p], out_recv.at[2]
            ).start()

    for index, ref in enumerate((gq_out, near_out, far_out)):
        got(ref, out_recv.at[index])

    got(kv_stage.at[:, :, pl.ds(0, (n - 1) * HEAD)], in_send.at[0])
    got(qc_stage.at[:, :, pl.ds(0, (n - 1) * wide)], in_send.at[1])
    got(dq_out.at[pl.ds(0, (n - 1) * rows), :], out_send.at[0])
    got(back_out.at[0, :, pl.ds(0, (n - 1) * rows), :], out_send.at[1])

    @pl.when(chip > 0)
    def _():
        got(back_out.at[1], out_send.at[2])

    for step in range(FAR + 1):
        @pl.when(chip >= step)
        def _():
            for piece in pieces:
                share(piece, step).wait_send()
                if step > 1:
                    back(piece, step).wait_send()

        if step < FAR:
            @pl.when((chip >= step) & (chip < last))
            def _():
                for piece in pieces:
                    forward(piece, step).wait_send()

    for step in range(FAR + 1):
        @pl.when(gives(step))
        def _():
            hand_over(step).wait_send()


def finish(gq_in, near_in, far_in, gq_out, gk_out, gv_out, gq_blk, parts, sums, sems):
    n, rows, wide = gq_in.shape

    def queries_of(p):
        return pltpu.make_async_copy(
            gq_in.at[p], gq_blk.at[:, p * wide : (p + 1) * wide], sems.at[0]
        )

    loads = [
        pltpu.make_async_copy(src, parts.at[i], sems.at[1 + i])
        for i, src in enumerate((near_in, far_in))
    ]
    for load in loads:
        load.start()
    for p in range(n):
        queries_of(p).start()
    for load in loads:
        load.wait()
    stores = []
    for index, (dst, factor) in enumerate(((gk_out, HEAD ** -0.5), (gv_out, 1.0))):
        for p in range(n):
            total = parts[0, p, index].astype(jnp.float32) + parts[1, p, index].astype(jnp.float32)
            sums[index, :, p * HEAD : (p + 1) * HEAD] = (total * factor).astype(jnp.bfloat16)
        stores.append(pltpu.make_async_copy(sums.at[index], dst, sems.at[3 + index]))
        stores[-1].start()
    pltpu.make_async_copy(gq_blk, gq_blk, sems.at[0]).wait()
    stores.append(pltpu.make_async_copy(gq_blk, gq_out, sems.at[5]))
    stores[-1].start()
    for store in stores:
        store.wait()


def shards(queries, keys, values, grad_out, doc_lengths):
    n = lax.axis_size("tp")
    rows = queries.shape[0]
    block = rows * n
    wide = queries.shape[1] // n
    group = wide // HEAD
    blocks = 2 * FAR + 1
    bf16, f32 = jnp.bfloat16, jnp.float32
    vmem = pltpu.VMEM
    dma = pltpu.SemaphoreType.DMA
    any_spec = pl.BlockSpec(memory_space=pl.ANY)
    like_q = jax.ShapeDtypeStruct(queries.shape, bf16)
    like_k = jax.ShapeDtypeStruct(keys.shape, bf16)
    split_q = jax.ShapeDtypeStruct((n, rows, wide), bf16)
    split_kv = jax.ShapeDtypeStruct((n, 2, rows, HEAD), bf16)
    parts = pl.pallas_call(
        kernel,
        out_shape=[split_q] + [split_kv] * 2,
        in_specs=[any_spec] * 4 + [pl.BlockSpec(memory_space=pltpu.SMEM)],
        out_specs=[any_spec] * 3,
        scratch_shapes=[
            vmem((2, *queries.shape), bf16),
            vmem((2, *keys.shape), bf16),
            vmem((2, block, wide), bf16),
            vmem((2 * FAR + 2, 2, block, HEAD), bf16),
            vmem((blocks * group, block, block), f32),
            vmem((blocks * group, block, block), f32),
            vmem((blocks * group, 1, block), f32),
            vmem((1, block), jnp.int32),
            vmem((group, HEAD, block), f32),
            vmem((block, wide), bf16),
            vmem((FAR + 1, 2, block, HEAD), f32),
            vmem((FAR + 1, 2, block, HEAD), bf16),
            vmem((FAR + 1, 2, block, HEAD), bf16),
            vmem((FAR + 1, 2, block, HEAD), bf16),
            vmem((FAR, 2, block, HEAD), bf16),
            dma((4,)),
            dma((2,)),
            dma((2,)),
            dma((FAR, 2, HALVES)),
            dma((FAR, 2, HALVES)),
            dma((FAR + 1, 2, HALVES)),
            dma((FAR + 1, 2, HALVES)),
            dma((FAR, 2, HALVES)),
            dma((FAR, 2, HALVES)),
            dma((FAR + 1,)),
            dma((FAR + 1,)),
            dma((3,)),
            dma((3,)),
        ],
        compiler_params=pltpu.CompilerParams(
            collective_id=0, has_side_effects=True, vmem_limit_bytes=60 * 2**20
        ),
    )(queries, keys, values, grad_out, doc_lengths)
    return pl.pallas_call(
        finish,
        out_shape=[like_q, like_k, like_k],
        in_specs=[any_spec] * 3,
        out_specs=[any_spec] * 3,
        scratch_shapes=[
            vmem(queries.shape, bf16),
            vmem((2, n, 2, rows, HEAD), bf16),
            vmem((2, *keys.shape), bf16),
            dma((6,)),
        ],
        compiler_params=pltpu.CompilerParams(vmem_limit_bytes=60 * 2**20),
    )(*parts)


def solution(mesh):
    placed = P(("ctx", "tp"), None)
    return jax.shard_map(
        shards,
        mesh=mesh,
        in_specs=(placed,) * 4 + (P(),),
        out_specs=(placed,) * 3,
        check_vma=False,
    )
```

time: 66.2 us -> 63.1 us (0.953)
  the two profiles are of different devices: /device:TPU:1 before, /device:TPU:6 now
where the time goes in v3:
time: 63.1 us; the launch traced here: 62.9 us
  Pallas kernels  62.3 us (99%)
  between operations  0.64 us (1%)
    pallas_call x1, Pallas kernels, shards(): pl.pallas_call(kernel, out_shape=[split_q] + [split_kv] * 2, in_specs=[an...  60.5 us
    pallas_call x1, Pallas kernels, shards(): pl.pallas_call(finish, out_shape=[like_q, like_k, like_k], in_specs=[any_...  1.79 us

profile of v3, /device:TPU:6, one launch (start us, length us, event | category | flops | bytes accessed | tf_op | source)
XLA Modules:
  0.0 62.9 jit_solution(1411964657285087274)
XLA Ops:
  0.6 60.5 %shard_map.76 = (bf16[8,32,512]{2,1,0:T(8,128)(2,1)}, bf16[8,2,32,128]{3,2,1,0:T(8,128)(2,1)}, bf16[8,2,32,128]{3,2,1,0:T(8,128)(2,1)}) custom-call(bf16[32,4096]{1,0:T(8,128)(2,1)} %q_in.1, bf16[32,1024]{1,0:T(8,128)(2,1)} %k_in.1, bf16[32,1024]{1,0:T(8,128)(2,1)} %v_in.1, bf16[32,4096]{1,0:T(8,128)(2,1)} %c_in.1, s32[24]{0:T(128)} %lengths.1), custom_call_target="tpu_custom_call" | custom-call | tf_op jit(solution)/shard_map/pallas_call | solution.py:438
  61.1 1.8 %shard_map.77 = (bf16[32,4096]{1,0:T(8,128)(2,1)}, bf16[32,1024]{1,0:T(8,128)(2,1)}, bf16[32,1024]{1,0:T(8,128)(2,1)}) custom-call(bf16[8,32,512]{2,1,0:T(8,128)(2,1)} %get-tuple-element.6.gq_in, bf16[8,2,32,128]{3,2,1,0:T(8,128)(2,1)} %get-tuple-element.7.near_in, bf16[8,2,32,128]{3,2,1,0:T(8,128)(2,1)} %get-tuple-element.8.far_in), custom_call_target="tpu_custom_call" | custom-call | tf_op jit(solution)/shard_map/pallas_call | solution.py:477

commit v4 on v3

--- a/solution.py
+++ b/solution.py
@@ -1,3 +1,5 @@
+import functools
+
 import jax
 import jax.numpy as jnp
 from jax import lax
@@ -24,7 +26,7 @@
     gq_out, near_out, far_out,
     qc_stage, kv_stage, qc_blk, kv_win, weights, dprobs, tops, starts,
     dq_acc, dq_out, own, sib_out, sib_in, back_out, back_in,
-    stage_sem, in_send, in_recv, fwd_send, fwd_recv, pair_send, pair_recv,
+    stage_sem, home_sem, in_send, in_recv, fwd_send, fwd_recv, pair_send, pair_recv,
     back_send, back_recv, term_send, term_recv, out_send, out_recv,
 ):
     n = lax.axis_size("tp")
@@ -52,6 +54,9 @@
         pl.semaphore_signal(
             barrier, inc=1, device_id=(me, lax.rem(y + o, n)), device_id_type=MESH
         )
+        pl.semaphore_signal(
+            barrier, inc=1, device_id=(before, lax.rem(y + o, n)), device_id_type=MESH
+        )
     for other in (before, twin):
         pl.semaphore_signal(barrier, inc=1, device_id=(other, y), device_id_type=MESH)
 
@@ -87,27 +92,38 @@
 
     for index, (src, dst) in enumerate(staged):
         pltpu.make_async_copy(src, dst, stage_sem.at[index]).wait()
-    pl.semaphore_wait(barrier, n + 1)
+    pl.semaphore_wait(barrier, 2 * n)
 
     here = pl.ds(pl.multiple_of(y * rows, rows), rows)
 
-    def spread(index, src, width, dst):
+    def spread(index, src, width, dst, to_ctx, others):
         def of(p):
             return src.at[:, :, pl.ds(pl.multiple_of(p * width, width), width)]
 
-        for o in offsets:
+        for o in others:
             to = lax.rem(y + o, n)
             pltpu.make_async_remote_copy(
                 src_ref=of(to),
                 dst_ref=dst,
                 send_sem=in_send.at[index],
                 recv_sem=in_recv.at[index],
-                device_id=(me, to),
+                device_id=(to_ctx, to),
                 device_id_type=MESH,
             ).start()
-        pltpu.make_async_copy(of(y), dst, in_recv.at[index]).start()
-
-    spread(0, kv_stage, HEAD, kv_win.at[mine, :, here, :])
+        if 0 not in others:
+            pltpu.make_async_copy(of(y), dst, in_recv.at[index]).start()
+
+    @pl.when(chip < last)
+    def _():
+        spread(2, kv_stage, HEAD, kv_win.at[mine + 2, :, here, :], after, offsets + [0])
+
+    @pl.when(chip == last)
+    def _():
+        spread(0, kv_stage, HEAD, kv_win.at[mine, :, here, :], me, offsets)
+
+    def side_sem(h):
+        return 1 if h < group // 2 else 3
+
     for h in range(group):
         for o in offsets + [0]:
             to = lax.rem(y + o, n)
@@ -115,11 +131,15 @@
             dst = qc_blk.at[:, here, h * HEAD : (h + 1) * HEAD]
             if o:
                 pltpu.make_async_remote_copy(
-                    src_ref=src, dst_ref=dst, send_sem=in_send.at[1], recv_sem=in_recv.at[1],
-                    device_id=(me, to), device_id_type=MESH,
+                    src_ref=src,
+                    dst_ref=dst,
+                    send_sem=in_send.at[side_sem(h)],
+                    recv_sem=in_recv.at[side_sem(h)],
+                    device_id=(me, to),
+                    device_id_type=MESH,
                 ).start()
             else:
-                pltpu.make_async_copy(src, dst, in_recv.at[1]).start()
+                pltpu.make_async_copy(src, dst, in_recv.at[side_sem(h)]).start()
 
     def got(ref, sem):
         pltpu.make_async_copy(ref, ref, sem).wait()
@@ -155,8 +175,11 @@
     def relay(step):
         @pl.when(chip >= step)
         def _():
+            if step == 1:
+                got(kv_win.at[mine + 2], in_recv.at[2])
             for piece in pieces:
-                forward(piece, step - 1).wait_recv()
+                if step > 1:
+                    forward(piece, step - 1).wait_recv()
                 if step < FAR:
                     @pl.when(chip < last)
                     def _():
@@ -164,6 +187,16 @@
 
                 share(piece, step).start()
 
+    def give_back():
+        return pltpu.make_async_remote_copy(
+            src_ref=kv_win.at[mine + 2],
+            dst_ref=kv_win.at[mine],
+            send_sem=home_sem.at[0],
+            recv_sem=home_sem.at[1],
+            device_id=(before, y),
+            device_id_type=MESH,
+        )
+
     def shared(step):
         @pl.when(chip >= step)
         def _():
@@ -173,58 +206,76 @@
     def of_head(index, h):
         return qc_blk[index, :, h * HEAD : (h + 1) * HEAD]
 
-    def scan_block(far, carry, diagonal=False):
-        at = far + mine
-        k = kv_win[at, 0]
-        v = kv_win[at, 1]
-        allowed = key_row >= starts[...] - (me - far) * block
-        if diagonal:
-            allowed = allowed & (key_row <= query_lane)
+    def scan_blocks(fars, heads, carry, diagonal=False):
+        allowed = []
+        for far in fars:
+            inside = key_row >= starts[...] - (me - far) * block
+            allowed.append(inside & (key_row <= query_lane) if diagonal else inside)
         new = []
-        for h in range(group):
-            s = dot(k, of_head(0, h), NT)
-            dp = dot(v, of_head(1, h), NT)
-            s = jnp.where(allowed, s, LOW)
-            top = jnp.max(s, axis=0, keepdims=True)
+        for j, h in enumerate(heads):
+            scores = []
+            for far, inside in zip(fars, allowed):
+                s = dot(kv_win[far + mine, 0], of_head(0, h), NT)
+                scores.append(jnp.where(inside, s, LOW))
+            tops_here = [jnp.max(s, axis=0, keepdims=True) for s in scores]
             if not diagonal:
-                top = jnp.maximum(top, carry[h][0])
-            e = jnp.exp2(s * scale - top * scale)
-            total = jnp.sum(e, axis=0, keepdims=True)
-            weighted = jnp.sum(e * dp, axis=0, keepdims=True)
+                tops_here.append(carry[j][0])
+            top = functools.reduce(jnp.maximum, tops_here)
+            total = jnp.zeros((1, block), jnp.float32)
+            weighted = jnp.zeros((1, block), jnp.float32)
             if not diagonal:
-                old, old_total, old_weighted = carry[h]
+                old, total, weighted = carry[j]
                 shrink = jnp.exp2((old - top) * scale)
-                total = total + old_total * shrink
-                weighted = weighted + old_weighted * shrink
-            weights[far * group + h] = e
-            dprobs[far * group + h] = dp
-            tops[far * group + h] = top
+                total = total * shrink
+                weighted = weighted * shrink
+            for far, s in zip(fars, scores):
+                dp = dot(kv_win[far + mine, 1], of_head(1, h), NT)
+                e = jnp.exp2(s * scale - top * scale)
+                total = total + jnp.sum(e, axis=0, keepdims=True)
+                weighted = weighted + jnp.sum(e * dp, axis=0, keepdims=True)
+                weights[far * group + h] = e
+                dprobs[far * group + h] = dp
+                tops[far * group + h] = top
             new.append((top, total, weighted))
         return tuple(new)
 
-    def scan(first, last, carry):
-        return lax.fori_loop(first, last + 1, scan_block, carry)
-
-    got(kv_win.at[mine], in_recv.at[0])
+    def scan_side(heads):
+        carry = scan_blocks((0,), heads, None, True)
+        return lax.fori_loop(
+            0, FAR - 1, lambda i, c: scan_blocks((2 * i + 1, 2 * i + 2), heads, c), carry
+        )
+
+    relay(1)
+
+    @pl.when(chip > 0)
+    def _():
+        give_back().start()
+
+    relay(2)
 
     @pl.when(chip < last)
     def _():
-        for piece in pieces:
-            forward(piece, 0).start()
+        give_back().wait_recv()
+
+    @pl.when(chip == last)
+    def _():
+        got(kv_win.at[mine], in_recv.at[0])
 
     for piece in pieces:
         share(piece, 0).start()
-    for step in range(1, FAR):
-        relay(step)
-    got(qc_blk, in_recv.at[1])
-    stats = scan_block(0, None, True)
+    relay(3)
     for step in range(FAR):
         shared(step)
-    stats = scan(1, 2 * FAR - 2, stats)
+    stats = ()
+    for side in range(2):
+        heads = tuple(range(side * group // 2, (side + 1) * group // 2))
+        sem = in_recv.at[side_sem(heads[0])]
+        got(qc_blk.at[:, :, heads[0] * HEAD : (heads[-1] + 1) * HEAD], sem)
+        stats += scan_side(heads)
     relay(FAR)
-    stats = scan_block(2 * FAR, stats)
+    stats = scan_blocks((2 * FAR,), range(group), stats)
     shared(FAR)
-    stats = scan_block(2 * FAR - 1, stats)
+    stats = scan_blocks((2 * FAR - 1,), range(group), stats)
 
     def terms(far):
         at = far + mine
@@ -359,8 +410,20 @@
     for index, ref in enumerate((gq_out, near_out, far_out)):
         got(ref, out_recv.at[index])
 
-    got(kv_stage.at[:, :, pl.ds(0, (n - 1) * HEAD)], in_send.at[0])
-    got(qc_stage.at[:, :, pl.ds(0, (n - 1) * wide)], in_send.at[1])
+    @pl.when(chip == last)
+    def _():
+        got(kv_stage.at[:, :, pl.ds(0, (n - 1) * HEAD)], in_send.at[0])
+
+    @pl.when(chip > 0)
+    def _():
+        give_back().wait_send()
+
+    @pl.when(chip < last)
+    def _():
+        got(kv_stage, in_send.at[2])
+
+    for index in (1, 3):
+        got(qc_stage.at[:, :, pl.ds(0, (n - 1) * wide // 2)], in_send.at[index])
     got(dq_out.at[pl.ds(0, (n - 1) * rows), :], out_send.at[0])
     got(back_out.at[0, :, pl.ds(0, (n - 1) * rows), :], out_send.at[1])
 
@@ -376,7 +439,7 @@
                 if step > 1:
                     back(piece, step).wait_send()
 
-        if step < FAR:
+        if 0 < step < FAR:
             @pl.when((chip >= step) & (chip < last))
             def _():
                 for piece in pieces:
@@ -458,7 +521,8 @@
             vmem((FAR, 2, block, HEAD), bf16),
             dma((4,)),
             dma((2,)),
-            dma((2,)),
+            dma((4,)),
+            dma((4,)),
             dma((FAR, 2, HALVES)),
             dma((FAR, 2, HALVES)),
             dma((FAR + 1, 2, HALVES)),

time: 63.1 us -> 61.6 us (0.976)
  Pallas kernels: 62.3 us -> 60.8 us
    pallas_call x1, Pallas kernels: 60.5 us -> 59 us  [shards(): pl.pallas_call(kernel, out_shape=[split_q] + [split_kv] * 2, in_specs=[an...]
where the time goes in v4:
time: 61.6 us; the launch traced here: 61.4 us
  Pallas kernels  60.8 us (99%)
  between operations  0.64 us (1%)
    pallas_call x1, Pallas kernels, shards(): pl.pallas_call(kernel, out_shape=[split_q] + [split_kv] * 2, in_specs=[an...  59 us
    pallas_call x1, Pallas kernels, shards(): pl.pallas_call(finish, out_shape=[like_q, like_k, like_k], in_specs=[any_...  1.79 us

profile of v4, /device:TPU:6, one launch (start us, length us, event | category | flops | bytes accessed | tf_op | source)
XLA Modules:
  0.0 61.4 jit_solution(5984668765388833518)
XLA Ops:
  0.6 59.0 %shard_map.76 = (bf16[8,32,512]{2,1,0:T(8,128)(2,1)}, bf16[8,2,32,128]{3,2,1,0:T(8,128)(2,1)}, bf16[8,2,32,128]{3,2,1,0:T(8,128)(2,1)}) custom-call(bf16[32,4096]{1,0:T(8,128)(2,1)} %q_in.1, bf16[32,1024]{1,0:T(8,128)(2,1)} %k_in.1, bf16[32,1024]{1,0:T(8,128)(2,1)} %v_in.1, bf16[32,4096]{1,0:T(8,128)(2,1)} %c_in.1, s32[24]{0:T(128)} %lengths.1), custom_call_target="tpu_custom_call" | custom-call | tf_op jit(solution)/shard_map/pallas_call | solution.py:501
  59.6 1.8 %shard_map.77 = (bf16[32,4096]{1,0:T(8,128)(2,1)}, bf16[32,1024]{1,0:T(8,128)(2,1)}, bf16[32,1024]{1,0:T(8,128)(2,1)}) custom-call(bf16[8,32,512]{2,1,0:T(8,128)(2,1)} %get-tuple-element.6.gq_in, bf16[8,2,32,128]{3,2,1,0:T(8,128)(2,1)} %get-tuple-element.7.near_in, bf16[8,2,32,128]{3,2,1,0:T(8,128)(2,1)} %get-tuple-element.8.far_in), custom_call_target="tpu_custom_call" | custom-call | tf_op jit(solution)/shard_map/pallas_call | solution.py:541

commit v5 on v4

--- a/solution.py
+++ b/solution.py
@@ -23,11 +23,11 @@
 
 def kernel(
     q_in, k_in, v_in, c_in, lengths,
-    gq_out, near_out, far_out,
+    gq_out, gkv_out,
     qc_stage, kv_stage, qc_blk, kv_win, weights, dprobs, tops, starts,
-    dq_acc, dq_out, own, sib_out, sib_in, back_out, back_in,
+    dq_acc, dq_out, own, sib_acc, sib_out, sib_in, back_out, back_in, ahead_in,
     stage_sem, home_sem, in_send, in_recv, fwd_send, fwd_recv, pair_send, pair_recv,
-    back_send, back_recv, term_send, term_recv, out_send, out_recv,
+    back_send, back_recv, ahead_send, ahead_recv, term_send, term_recv, out_send, out_recv,
 ):
     n = lax.axis_size("tp")
     ring = lax.axis_size("ctx")
@@ -38,6 +38,7 @@
     last = ring // 2 - 1
     after = lax.rem(me + 2, ring)
     before = lax.rem(me + ring - 2, ring)
+    source = lax.rem(me + ring - 4, ring)
     twin = me + 1 - 2 * core
     rows = q_in.shape[0]
     block = rows * n
@@ -267,8 +268,8 @@
     for step in range(FAR):
         shared(step)
     stats = ()
-    for side in range(2):
-        heads = tuple(range(side * group // 2, (side + 1) * group // 2))
+    sides = [tuple(range(i * group // 2, (i + 1) * group // 2)) for i in range(2)]
+    for heads in sides:
         sem = in_recv.at[side_sem(heads[0])]
         got(qc_blk.at[:, :, heads[0] * HEAD : (heads[-1] + 1) * HEAD], sem)
         stats += scan_side(heads)
@@ -277,12 +278,12 @@
     shared(FAR)
     stats = scan_blocks((2 * FAR - 1,), range(group), stats)
 
-    def terms(far):
+    def terms(far, heads):
         at = far + mine
         k_t = kv_win[at, 0].T
         dk = jnp.zeros((block, HEAD), jnp.float32)
         dv = jnp.zeros((block, HEAD), jnp.float32)
-        for h in range(group):
+        for h in heads:
             top, total, weighted = stats[h]
             inv = 1.0 / total
             shrink = jnp.exp2((tops[far * group + h] - top) * scale) * inv
@@ -324,11 +325,11 @@
     def make_terms(step):
         @pl.when(gives(step))
         def _():
-            for index, term in enumerate(terms(2 * step - 1 + 2 * core)):
+            for index, term in enumerate(terms(2 * step - 1 + 2 * core, range(group))):
                 sib_out[step, index] = term.astype(jnp.bfloat16)
             hand_over(step).start()
 
-        for index, term in enumerate(terms(2 * step)):
+        for index, term in enumerate(terms(2 * step, range(group))):
             own[step, index] = term
 
     def take(step):
@@ -337,77 +338,149 @@
             hand_over(step).wait_recv()
             own[step] += sib_in[step].astype(jnp.float32)
 
+    def ahead(piece, step):
+        index, part = piece
+        span = pl.ds(part * half, half)
+        return pltpu.make_async_remote_copy(
+            src_ref=back_out.at[step, index, span],
+            dst_ref=ahead_in.at[step, index, span],
+            send_sem=ahead_send.at[step, index, part],
+            recv_sem=ahead_recv.at[step, index, part],
+            device_id=(after, y),
+            device_id_type=MESH,
+        )
+
+    def added(piece, step, *more):
+        index, part = piece
+        span = pl.ds(part * half, half)
+        sums = own[step, index, span]
+        for ref in more:
+            sums = sums + ref[index, span].astype(jnp.float32)
+        if step in (0, 2) and index == 0:
+            sums = sums * factor
+        back_out[step, index, span] = sums.astype(jnp.bfloat16)
+
     def pass_on(step):
         @pl.when(chip >= step)
         def _():
-            for index, part in pieces:
-                span = pl.ds(part * half, half)
-                sums = own[step, index, span]
+            for piece in pieces:
                 if step < FAR:
                     @pl.when(chip < last)
                     def _():
-                        back((index, part), step + 1).wait_recv()
-
-                    sums = sums + back_in[step, index, span].astype(jnp.float32)
-                back_out[step, index, span] = sums.astype(jnp.bfloat16)
-                if step > 1:
-                    back((index, part), step).start()
+                        back(piece, step + 1).wait_recv()
+
+                    added(piece, step, back_in.at[step])
+                else:
+                    added(piece, step)
+                back(piece, step).start()
+
+    def pass_ahead_0():
+        @pl.when(chip < last - 1)
+        def _():
+            for index, part in pieces:
+                span = pl.ds(part * half, half)
+                back_out[0, index, span] = own[0, index, span].astype(jnp.bfloat16)
+                ahead((index, part), 0).start()
+
+    def pass_ahead_1():
+        @pl.when((chip >= 1) & (chip < last))
+        def _():
+            for piece in pieces:
+                ahead(piece, 0).wait_recv()
+                added(piece, 1, ahead_in.at[0])
+                ahead(piece, 1).start()
+
+        @pl.when(chip == last)
+        def _():
+            for piece in pieces:
+                added(piece, 1)
+                back(piece, 1).start()
 
     def make_step(i, carry):
-        step = FAR - i
-        make_terms(step)
-
-        @pl.when(step == FAR - 1)
-        def _():
-            take(FAR)
-            pass_on(FAR)
-
+        make_terms(FAR * (1 - i))
         return carry
 
-    def deliver(index, src, dst, to_ctx, others):
+    def make_side(side):
+        heads = sides[side]
+
+        def step_of(i, carry):
+            step = jnp.where(i == 0, 3, i)
+            other = terms(2 * step - 1 + 2 * core, heads)
+            same = terms(2 * step, heads)
+            for index in range(2):
+                if side == 0:
+                    sib_acc[step, index] = other[index]
+                    own[step, index] = same[index]
+                else:
+                    sib_out[step, index] = (sib_acc[step, index] + other[index]).astype(jnp.bfloat16)
+                    own[step, index] += same[index]
+            if side == 1:
+                hand_over(step).start()
+            return carry
+
+        lax.fori_loop(0, 3, step_of, 0)
+        for h in heads:
+            dq_out[side, :, (h - heads[0]) * HEAD : (h - heads[0] + 1) * HEAD] = (
+                (dq_acc[h] * factor).T.astype(jnp.bfloat16)
+            )
+
+    def deliver(index, src, dst, to_ctx, others, side=None):
         def at(p):
             rows_of = pl.ds(pl.multiple_of(p * rows, rows), rows)
             return src.at[:, rows_of, :] if len(src.shape) == 3 else src.at[rows_of, :]
 
+        there = dst.at[y] if side is None else dst.at[y, side]
         for o in others:
             to = lax.rem(y + o, n)
             pltpu.make_async_remote_copy(
                 src_ref=at(to),
-                dst_ref=dst.at[y],
+                dst_ref=there,
                 send_sem=out_send.at[index],
-                recv_sem=out_recv.at[index],
+                recv_sem=out_recv.at[index % 3 and 1],
                 device_id=(to_ctx, to),
                 device_id_type=MESH,
             ).start()
         if 0 not in others:
-            pltpu.make_async_copy(at(y), dst.at[y], out_recv.at[index]).start()
-
-    lax.fori_loop(0, FAR + 1, make_step, 0)
+            pltpu.make_async_copy(at(y), there, out_recv.at[index % 3 and 1]).start()
+
+    lax.fori_loop(0, 2, make_step, 0)
+    take(FAR)
+    pass_on(FAR)
+    take(0)
+    pass_ahead_0()
+    make_side(0)
+    deliver(0, dq_out.at[0], gq_out, me, offsets, 0)
+    make_side(1)
     take(3)
     pass_on(3)
-    for h in range(group):
-        dq_out[:, h * HEAD : (h + 1) * HEAD] = (dq_acc[h] * factor).T.astype(jnp.bfloat16)
-    deliver(0, dq_out, gq_out, me, offsets)
-    take(0)
-    back_out[0] = own[0].astype(jnp.bfloat16)
-    deliver(1, back_out.at[0], near_out, me, offsets)
+    take(1)
+    pass_ahead_1()
+    deliver(3, dq_out.at[1], gq_out, me, offsets, 1)
     take(2)
-    pass_on(2)
-    take(1)
-    pass_on(1)
-
-    @pl.when(chip > 0)
-    def _():
-        deliver(2, back_out.at[1], far_out, before, offsets + [0])
-
-    @pl.when(chip == last)
-    def _():
-        for p in range(n):
-            pltpu.make_async_copy(
-                back_in.at[0, :, p * rows : (p + 1) * rows], far_out.at[p], out_recv.at[2]
-            ).start()
-
-    for index, ref in enumerate((gq_out, near_out, far_out)):
+
+    @pl.when(chip >= 2)
+    def _():
+        for piece in pieces:
+            ahead(piece, 1).wait_recv()
+
+            @pl.when(chip < last)
+            def _():
+                back(piece, 3).wait_recv()
+
+            added(piece, 2, ahead_in.at[1], back_in.at[2])
+        deliver(1, back_out.at[2], gkv_out, source, offsets + [0])
+
+    @pl.when(chip >= last - 1)
+    def _():
+        for piece in pieces:
+            @pl.when(chip == last - 1)
+            def _():
+                back(piece, 1).wait_recv()
+
+            added(piece, 0, back_in.at[0])
+        deliver(2, back_out.at[0], gkv_out, me, offsets)
+
+    for index, ref in enumerate((gq_out, gkv_out)):
         got(ref, out_recv.at[index])
 
     @pl.when(chip == last)
@@ -424,19 +497,38 @@
 
     for index in (1, 3):
         got(qc_stage.at[:, :, pl.ds(0, (n - 1) * wide // 2)], in_send.at[index])
-    got(dq_out.at[pl.ds(0, (n - 1) * rows), :], out_send.at[0])
-    got(back_out.at[0, :, pl.ds(0, (n - 1) * rows), :], out_send.at[1])
-
-    @pl.when(chip > 0)
-    def _():
-        got(back_out.at[1], out_send.at[2])
+    for side in range(2):
+        got(dq_out.at[side, pl.ds(0, (n - 1) * rows), :], out_send.at[3 * side])
+
+    @pl.when(chip >= 2)
+    def _():
+        got(back_out.at[2], out_send.at[1])
+
+    @pl.when(chip >= last - 1)
+    def _():
+        got(back_out.at[0, :, pl.ds(0, (n - 1) * rows), :], out_send.at[2])
+
+    @pl.when(chip < last - 1)
+    def _():
+        for piece in pieces:
+            ahead(piece, 0).wait_send()
+
+    @pl.when((chip >= 1) & (chip < last))
+    def _():
+        for piece in pieces:
+            ahead(piece, 1).wait_send()
+
+    @pl.when(chip == last)
+    def _():
+        for piece in pieces:
+            back(piece, 1).wait_send()
 
     for step in range(FAR + 1):
         @pl.when(chip >= step)
         def _():
             for piece in pieces:
                 share(piece, step).wait_send()
-                if step > 1:
+                if step > 2:
                     back(piece, step).wait_send()
 
         if 0 < step < FAR:
@@ -451,34 +543,28 @@
             hand_over(step).wait_send()
 
 
-def finish(gq_in, near_in, far_in, gq_out, gk_out, gv_out, gq_blk, parts, sums, sems):
-    n, rows, wide = gq_in.shape
-
-    def queries_of(p):
-        return pltpu.make_async_copy(
-            gq_in.at[p], gq_blk.at[:, p * wide : (p + 1) * wide], sems.at[0]
-        )
-
-    loads = [
-        pltpu.make_async_copy(src, parts.at[i], sems.at[1 + i])
-        for i, src in enumerate((near_in, far_in))
+def finish(gq_in, gkv_in, gq_out, gk_out, gv_out, gq_blk, gkv_blk, load_sems, store_sems):
+    n, sides, rows, half = gq_in.shape
+    blocks = (gkv_blk.at[0], gkv_blk.at[1], gq_blk)
+    for p in range(n):
+        for index in range(2):
+            pltpu.make_async_copy(
+                gkv_in.at[p, index],
+                blocks[index].at[:, p * HEAD : (p + 1) * HEAD],
+                load_sems.at[index],
+            ).start()
+        for side in range(sides):
+            at = (p * sides + side) * half
+            pltpu.make_async_copy(
+                gq_in.at[p, side], gq_blk.at[:, at : at + half], load_sems.at[2]
+            ).start()
+    stores = [
+        pltpu.make_async_copy(blocks[index], dst, store_sems.at[index])
+        for index, dst in enumerate((gk_out, gv_out, gq_out))
     ]
-    for load in loads:
-        load.start()
-    for p in range(n):
-        queries_of(p).start()
-    for load in loads:
-        load.wait()
-    stores = []
-    for index, (dst, factor) in enumerate(((gk_out, HEAD ** -0.5), (gv_out, 1.0))):
-        for p in range(n):
-            total = parts[0, p, index].astype(jnp.float32) + parts[1, p, index].astype(jnp.float32)
-            sums[index, :, p * HEAD : (p + 1) * HEAD] = (total * factor).astype(jnp.bfloat16)
-        stores.append(pltpu.make_async_copy(sums.at[index], dst, sems.at[3 + index]))
-        stores[-1].start()
-    pltpu.make_async_copy(gq_blk, gq_blk, sems.at[0]).wait()
-    stores.append(pltpu.make_async_copy(gq_blk, gq_out, sems.at[5]))
-    stores[-1].start()
+    for index in range(3):
+        pltpu.make_async_copy(blocks[index], blocks[index], load_sems.at[index]).wait()
+        stores[index].start()
     for store in stores:
         store.wait()
 
@@ -496,13 +582,13 @@
     any_spec = pl.BlockSpec(memory_space=pl.ANY)
     like_q = jax.ShapeDtypeStruct(queries.shape, bf16)
     like_k = jax.ShapeDtypeStruct(keys.shape, bf16)
-    split_q = jax.ShapeDtypeStruct((n, rows, wide), bf16)
+    split_q = jax.ShapeDtypeStruct((n, 2, rows, wide // 2), bf16)
     split_kv = jax.ShapeDtypeStruct((n, 2, rows, HEAD), bf16)
     parts = pl.pallas_call(
         kernel,
-        out_shape=[split_q] + [split_kv] * 2,
+        out_shape=[split_q, split_kv],
         in_specs=[any_spec] * 4 + [pl.BlockSpec(memory_space=pltpu.SMEM)],
-        out_specs=[any_spec] * 3,
+        out_specs=[any_spec] * 2,
         scratch_shapes=[
             vmem((2, *queries.shape), bf16),
             vmem((2, *keys.shape), bf16),
@@ -513,12 +599,14 @@
             vmem((blocks * group, 1, block), f32),
             vmem((1, block), jnp.int32),
             vmem((group, HEAD, block), f32),
-            vmem((block, wide), bf16),
+            vmem((2, block, wide // 2), bf16),
             vmem((FAR + 1, 2, block, HEAD), f32),
+            vmem((FAR, 2, block, HEAD), f32),
             vmem((FAR + 1, 2, block, HEAD), bf16),
             vmem((FAR + 1, 2, block, HEAD), bf16),
             vmem((FAR + 1, 2, block, HEAD), bf16),
             vmem((FAR, 2, block, HEAD), bf16),
+            vmem((2, 2, block, HEAD), bf16),
             dma((4,)),
             dma((2,)),
             dma((4,)),
@@ -529,10 +617,12 @@
             dma((FAR + 1, 2, HALVES)),
             dma((FAR, 2, HALVES)),
             dma((FAR, 2, HALVES)),
+            dma((2, 2, HALVES)),
+            dma((2, 2, HALVES)),
             dma((FAR + 1,)),
             dma((FAR + 1,)),
-            dma((3,)),
-            dma((3,)),
+            dma((4,)),
+            dma((2,)),
         ],
         compiler_params=pltpu.CompilerParams(
             collective_id=0, has_side_effects=True, vmem_limit_bytes=60 * 2**20
@@ -541,13 +631,13 @@
     return pl.pallas_call(
         finish,
         out_shape=[like_q, like_k, like_k],
-        in_specs=[any_spec] * 3,
+        in_specs=[any_spec] * 2,
         out_specs=[any_spec] * 3,
         scratch_shapes=[
             vmem(queries.shape, bf16),
-            vmem((2, n, 2, rows, HEAD), bf16),
             vmem((2, *keys.shape), bf16),
-            dma((6,)),
+            dma((3,)),
+            dma((3,)),
         ],
         compiler_params=pltpu.CompilerParams(vmem_limit_bytes=60 * 2**20),
     )(*parts)

time: 61.6 us -> 59.5 us (0.966)
  Pallas kernels: 60.8 us -> 58.6 us
    pallas_call x1, Pallas kernels: 59 us -> 56.9 us  [shards(): pl.pallas_call(kernel, out_shape=[split_q, split_kv], in_specs=[any_spec]...]
where the time goes in v5:
time: 59.5 us; the launch traced here: 59.3 us
  Pallas kernels  58.6 us (98%)
  between operations  0.64 us (1%)
    pallas_call x1, Pallas kernels, shards(): pl.pallas_call(kernel, out_shape=[split_q, split_kv], in_specs=[any_spec]...  56.9 us
    pallas_call x1, Pallas kernels, shards(): pl.pallas_call(finish, out_shape=[like_q, like_k, like_k], in_specs=[any_...  1.73 us

profile of v5, /device:TPU:6, one launch (start us, length us, event | category | flops | bytes accessed | tf_op | source)
XLA Modules:
  0.0 59.3 jit_solution(9107538754319069449)
XLA Ops:
  0.6 56.9 %shard_map.76 = (bf16[8,2,32,256]{3,2,1,0:T(8,128)(2,1)}, bf16[8,2,32,128]{3,2,1,0:T(8,128)(2,1)}) custom-call(bf16[32,4096]{1,0:T(8,128)(2,1)} %q_in.1, bf16[32,1024]{1,0:T(8,128)(2,1)} %k_in.1, bf16[32,1024]{1,0:T(8,128)(2,1)} %v_in.1, bf16[32,4096]{1,0:T(8,128)(2,1)} %c_in.1, s32[24]{0:T(128)} %lengths.1), custom_call_target="tpu_custom_call" | custom-call | tf_op jit(solution)/shard_map/pallas_call | solution.py:587
  57.5 1.7 %shard_map.77 = (bf16[32,4096]{1,0:T(8,128)(2,1)}, bf16[32,1024]{1,0:T(8,128)(2,1)}, bf16[32,1024]{1,0:T(8,128)(2,1)}) custom-call(bf16[8,2,32,256]{3,2,1,0:T(8,128)(2,1)} %get-tuple-element.5.gq_in, bf16[8,2,32,128]{3,2,1,0:T(8,128)(2,1)} %get-tuple-element.6.gkv_in), custom_call_target="tpu_custom_call" | custom-call | tf_op jit(solution)/shard_map/pallas_call | solution.py:631

commit v6 on v5

--- a/solution.py
+++ b/solution.py
@@ -99,7 +99,8 @@
 
     def spread(index, src, width, dst, to_ctx, others):
         def of(p):
-            return src.at[:, :, pl.ds(pl.multiple_of(p * width, width), width)]
+            columns = pl.ds(pl.multiple_of(p * width, width), width)
+            return src.at[:, :, columns] if len(src.shape) == 3 else src.at[:, columns]
 
         for o in others:
             to = lax.rem(y + o, n)
@@ -116,7 +117,9 @@
 
     @pl.when(chip < last)
     def _():
-        spread(2, kv_stage, HEAD, kv_win.at[mine + 2, :, here, :], after, offsets + [0])
+        for index in range(2):
+            dst = kv_win.at[mine + 2, index, here, :]
+            spread(2 + 2 * index, kv_stage.at[index], HEAD, dst, after, offsets + [0])
 
     @pl.when(chip == last)
     def _():
@@ -176,9 +179,9 @@
     def relay(step):
         @pl.when(chip >= step)
         def _():
-            if step == 1:
-                got(kv_win.at[mine + 2], in_recv.at[2])
             for piece in pieces:
+                if step == 1 and piece[1] == 0:
+                    got(kv_win.at[mine + 2, piece[0]], in_recv.at[2 + 2 * piece[0]])
                 if step > 1:
                     forward(piece, step - 1).wait_recv()
                 if step < FAR:
@@ -468,7 +471,9 @@
                 back(piece, 3).wait_recv()
 
             added(piece, 2, ahead_in.at[1], back_in.at[2])
-        deliver(1, back_out.at[2], gkv_out, source, offsets + [0])
+            index, part = piece
+            if part == HALVES - 1:
+                deliver(1, back_out.at[2, index], gkv_out, source, offsets + [0], index)
 
     @pl.when(chip >= last - 1)
     def _():
@@ -493,7 +498,8 @@
 
     @pl.when(chip < last)
     def _():
-        got(kv_stage, in_send.at[2])
+        for index in range(2):
+            got(kv_stage.at[index], in_send.at[2 + 2 * index])
 
     for index in (1, 3):
         got(qc_stage.at[:, :, pl.ds(0, (n - 1) * wide // 2)], in_send.at[index])
@@ -609,8 +615,8 @@
             vmem((2, 2, block, HEAD), bf16),
             dma((4,)),
             dma((2,)),
-            dma((4,)),
-            dma((4,)),
+            dma((5,)),
+            dma((5,)),
             dma((FAR, 2, HALVES)),
             dma((FAR, 2, HALVES)),
             dma((FAR + 1, 2, HALVES)),

time: 59.5 us -> 58.1 us (0.976)
  Pallas kernels: 58.6 us -> 57.2 us
    pallas_call x1, Pallas kernels: 56.9 us -> 55.5 us  [shards(): pl.pallas_call(kernel, out_shape=[split_q, split_kv], in_specs=[any_spec]...]
where the time goes in v6:
time: 58.1 us; the launch traced here: 57.9 us
  Pallas kernels  57.2 us (98%)
  between operations  0.64 us (1%)
    pallas_call x1, Pallas kernels, shards(): pl.pallas_call(kernel, out_shape=[split_q, split_kv], in_specs=[any_spec]...  55.5 us
    pallas_call x1, Pallas kernels, shards(): pl.pallas_call(finish, out_shape=[like_q, like_k, like_k], in_specs=[any_...  1.73 us

profile of v6, /device:TPU:6, one launch (start us, length us, event | category | flops | bytes accessed | tf_op | source)
XLA Modules:
  0.0 57.9 jit_solution(14803389804496248417)
XLA Ops:
  0.6 55.5 %shard_map.76 = (bf16[8,2,32,256]{3,2,1,0:T(8,128)(2,1)}, bf16[8,2,32,128]{3,2,1,0:T(8,128)(2,1)}) custom-call(bf16[32,4096]{1,0:T(8,128)(2,1)} %q_in.1, bf16[32,1024]{1,0:T(8,128)(2,1)} %k_in.1, bf16[32,1024]{1,0:T(8,128)(2,1)} %v_in.1, bf16[32,4096]{1,0:T(8,128)(2,1)} %c_in.1, s32[24]{0:T(128)} %lengths.1), custom_call_target="tpu_custom_call" | custom-call | tf_op jit(solution)/shard_map/pallas_call | solution.py:593
  56.1 1.7 %shard_map.77 = (bf16[32,4096]{1,0:T(8,128)(2,1)}, bf16[32,1024]{1,0:T(8,128)(2,1)}, bf16[32,1024]{1,0:T(8,128)(2,1)}) custom-call(bf16[8,2,32,256]{3,2,1,0:T(8,128)(2,1)} %get-tuple-element.5.gq_in, bf16[8,2,32,128]{3,2,1,0:T(8,128)(2,1)} %get-tuple-element.6.gkv_in), custom_call_target="tpu_custom_call" | custom-call | tf_op jit(solution)/shard_map/pallas_call | solution.py:637

commit v7 on v6

--- a/solution.py
+++ b/solution.py
@@ -128,22 +128,25 @@
     def side_sem(h):
         return 1 if h < group // 2 else 3
 
-    for h in range(group):
+    pair = wide // 2
+    for side in range(2):
         for o in offsets + [0]:
             to = lax.rem(y + o, n)
-            src = qc_stage.at[:, :, pl.ds(pl.multiple_of(to * wide + h * HEAD, HEAD), HEAD)]
-            dst = qc_blk.at[:, here, h * HEAD : (h + 1) * HEAD]
-            if o:
-                pltpu.make_async_remote_copy(
-                    src_ref=src,
-                    dst_ref=dst,
-                    send_sem=in_send.at[side_sem(h)],
-                    recv_sem=in_recv.at[side_sem(h)],
-                    device_id=(me, to),
-                    device_id_type=MESH,
-                ).start()
-            else:
-                pltpu.make_async_copy(src, dst, in_recv.at[side_sem(h)]).start()
+            columns = pl.ds(pl.multiple_of(to * wide + side * pair, HEAD), pair)
+            for index in range(2):
+                src = qc_stage.at[index, :, columns]
+                dst = qc_blk.at[index, here, side * pair : (side + 1) * pair]
+                if o:
+                    pltpu.make_async_remote_copy(
+                        src_ref=src,
+                        dst_ref=dst,
+                        send_sem=in_send.at[1 + 2 * side],
+                        recv_sem=in_recv.at[1 + 2 * side],
+                        device_id=(me, to),
+                        device_id_type=MESH,
+                    ).start()
+                else:
+                    pltpu.make_async_copy(src, dst, in_recv.at[1 + 2 * side]).start()
 
     def got(ref, sem):
         pltpu.make_async_copy(ref, ref, sem).wait()

time: 58.1 us -> 58.7 us (1.010)
  Pallas kernels: 57.2 us -> 57.9 us
    pallas_call x1, Pallas kernels: 55.5 us -> 56.1 us  [shards(): pl.pallas_call(kernel, out_shape=[split_q, split_kv], in_specs=[any_spec]...]
where the time goes in v7:
time: 58.7 us; the launch traced here: 58.5 us
  Pallas kernels  57.9 us (99%)
  between operations  0.64 us (1%)
    pallas_call x1, Pallas kernels, shards(): pl.pallas_call(kernel, out_shape=[split_q, split_kv], in_specs=[any_spec]...  56.1 us
    pallas_call x1, Pallas kernels, shards(): pl.pallas_call(finish, out_shape=[like_q, like_k, like_k], in_specs=[any_...  1.73 us

profile of v7, /device:TPU:6, one launch (start us, length us, event | category | flops | bytes accessed | tf_op | source)
XLA Modules:
  0.0 58.5 jit_solution(9852017803630881529)
XLA Ops:
  0.6 56.1 %shard_map.76 = (bf16[8,2,32,256]{3,2,1,0:T(8,128)(2,1)}, bf16[8,2,32,128]{3,2,1,0:T(8,128)(2,1)}) custom-call(bf16[32,4096]{1,0:T(8,128)(2,1)} %q_in.1, bf16[32,1024]{1,0:T(8,128)(2,1)} %k_in.1, bf16[32,1024]{1,0:T(8,128)(2,1)} %v_in.1, bf16[32,4096]{1,0:T(8,128)(2,1)} %c_in.1, s32[24]{0:T(128)} %lengths.1), custom_call_target="tpu_custom_call" | custom-call | tf_op jit(solution)/shard_map/pallas_call | solution.py:596
  56.8 1.7 %shard_map.77 = (bf16[32,4096]{1,0:T(8,128)(2,1)}, bf16[32,1024]{1,0:T(8,128)(2,1)}, bf16[32,1024]{1,0:T(8,128)(2,1)}) custom-call(bf16[8,2,32,256]{3,2,1,0:T(8,128)(2,1)} %get-tuple-element.5.gq_in, bf16[8,2,32,128]{3,2,1,0:T(8,128)(2,1)} %get-tuple-element.6.gkv_in), custom_call_target="tpu_custom_call" | custom-call | tf_op jit(solution)/shard_map/pallas_call | solution.py:640
